TPU v7x, 512 devices: a whole 4x8x8 slice. The times are simulated.
512 devices in a mesh: grp: 4 (over x_hi, core), lat: 16 (over z, x_lo), lon: 8 (over y).
Axes of the slice: x: 4 (x_hi: 2, x_lo: 2; x = x_hi * 2 + x_lo), y: 8, z: 8, core: 2. Of those that a mesh axis runs over, the one named last changes fastest.
Arguments:
- aloft_gridpoint: bfloat16 [8, 128, 2592], P('grp', 'lat', 'lon'), may hold values from -6 to 6
- parallel_nodes: int32 [128], P('lat'), may hold values from 20 to 2592, as said below
- layer_pressure_share: float32 [8], P('grp'), may hold values from 0.1 to 1
- layer_sensitivity: float32 [8], P('grp'), may hold values from 0.05 to 0.5
- associated_polynomial_quadrature: bfloat16 [128, 640, 1280], P('lat', 'lon'), may hold values from -0.75 to 0.75
- marine_heat: float32 [16, 512, 1024], P('grp', 'lat', 'lon'), may hold values from -6 to 6
- water_indicator: int32 [512, 1024], P('lat', 'lon'), may hold values 0 or 1
- heat_feeding_panels: int32 [512, 8, 4], P('lat', 'lon'), may hold values from 0 to 55295
- heat_transfer_factors: bfloat16 [512, 8, 4, 6, 128], P('lat', 'lon'), may hold values from -1.25 to 1.25
- skin_warmth_feeding_panels: int32 [128, 432, 2], P('lat', 'lon'), may hold values from 0 to 4095
- skin_warmth_mapping_factors: bfloat16 [128, 432, 2, 6, 128], P('lat', 'lon'), may hold values from -0.375 to 0.375
Outputs:
- spectra: float32 [1280, 16, 640], P('lat', 'grp', 'lon')
- ocean_out: float32 [16, 512, 1024], P('grp', 'lat', 'lon')
Inputs may be any that keep to these rules, and one draw needn't show every extreme that they name: `parallel_nodes`: octahedral point counts 20 + 4 * min(g, G - 1 - g) of rising global latitudes g of a grid of G = 1288 latitudes, one latitude from each run of G // 128 of them; the first row is a polar one and one row lies at the equator.
All inputs are finite; a program needn't handle non-finite values. No bound on the sum of `water_indicator` on one device may be relied on, other than what follows from the above.
Results may differ from a plain program's by a relative error of at most 0.0046.
Values may be sent and summed in bfloat16 or wider, within the bound.
A program may use at most 128 MiB of HBM per device.

v0:
```python
import jax
import jax.numpy as jnp
from jax import lax
from jax.sharding import PartitionSpec as P

TWO_PI = 6.283185307179586
FLUX_RATE = 0.5
KAPPA = 0.2


def spread(value, axis, root):
    mine = lax.axis_index(axis) == root
    return lax.psum(jnp.where(mine, value, jnp.zeros_like(value)), axis)


def with_halo(block, sides, width):
    for axis, dim in sides:
        count = lax.axis_size(axis)
        forward = [(i, i + 1) for i in range(count - 1)]
        backward = [(target, source) for source, target in forward]
        low = lax.ppermute(
            lax.slice_in_dim(block, block.shape[dim] - width, None, axis=dim), axis, forward
        )
        high = lax.ppermute(lax.slice_in_dim(block, 0, width, axis=dim), axis, backward)
        block = jnp.concatenate([low, block, high], axis=dim)
    return block


def fourier_rows(values, count_pts, lon_ids, count):
    wave_ids = jnp.arange(count, dtype=jnp.int32)
    phases = lon_ids[:, None] * wave_ids[None, :] % count_pts
    angles = phases.astype(jnp.float32) * (TWO_PI / count_pts.astype(jnp.float32))
    usable = (lon_ids[:, None] < count_pts) & (2 * wave_ids[None, :] < count_pts)
    cosine = jnp.where(usable, jnp.cos(angles), 0.0).astype(jnp.bfloat16)
    sine = jnp.where(usable, -jnp.sin(angles), 0.0).astype(jnp.bfloat16)
    basis = jnp.concatenate([cosine, sine], axis=1)
    summed = jnp.dot(values, basis, preferred_element_type=jnp.float32) / count_pts.astype(
        jnp.float32
    )
    return summed.reshape(values.shape[0], 2, count).transpose(2, 0, 1)


def diffuse(field, wet):
    middle = field[:, 1:-1, 1:-1]
    wet_mid = wet[1:-1, 1:-1]
    total = jnp.zeros_like(middle)
    pairs = (
        (field[:, :-2, 1:-1], wet[:-2, 1:-1]),
        (field[:, 2:, 1:-1], wet[2:, 1:-1]),
        (field[:, 1:-1, :-2], wet[1:-1, :-2]),
        (field[:, 1:-1, 2:], wet[1:-1, 2:]),
    )
    for near_field, near_wet in pairs:
        total = total + near_wet * (near_field - middle)
    return middle + KAPPA * wet_mid * total


def per_device(
    aloft_gridpoint,
    parallel_nodes,
    layer_pressure_share,
    layer_sensitivity,
    associated_polynomial_quadrature,
    marine_heat,
    water_indicator,
    heat_feeding_panels,
    heat_transfer_factors,
    skin_warmth_feeding_panels,
    skin_warmth_mapping_factors,
):
    maximal_magnitude = lax.Precision.HIGHEST
    lon_slot = lax.axis_index("lon")
    level_stack = aloft_gridpoint.shape[0]
    lat_count = aloft_gridpoint.shape[1]
    lon_local = aloft_gridpoint.shape[2]
    block_air = heat_transfer_factors.shape[3]
    marine_panel_array = heat_transfer_factors.shape[4]
    m_local = associated_polynomial_quadrature.shape[1]
    lon_ids = lon_slot * lon_local + jnp.arange(lon_local, dtype=jnp.int32)
    live = (lon_ids[None, :] < parallel_nodes[:, None]).astype(jnp.float32)
    aloft_state = aloft_gridpoint.astype(jnp.float32)
    partial_flux = jnp.sum(layer_pressure_share[:, None, None] * aloft_state, axis=0)
    column_flux = lax.psum(partial_flux, "grp") * live
    band_flux = lax.all_gather(column_flux, "lon", axis=1, tiled=True)
    whole_flux = lax.all_gather(band_flux.astype(jnp.bfloat16), "lat", axis=0, tiled=True).astype(
        band_flux.dtype
    )
    picked_air = jnp.take(
        whole_flux.reshape(-1, block_air), heat_feeding_panels.reshape(-1), axis=0
    ).reshape(heat_feeding_panels.shape + (block_air,))
    sea_top = spread(marine_heat[0], "grp", 0)
    band_sea = lax.all_gather(sea_top, "lon", axis=1, tiled=True)
    entire_ocean_field = lax.all_gather(band_sea, "lat", axis=0, tiled=True)
    selected_elements = jnp.take(
        entire_ocean_field.reshape(-1, marine_panel_array),
        skin_warmth_feeding_panels.reshape(-1),
        axis=0,
    ).reshape(skin_warmth_feeding_panels.shape + (marine_panel_array,))
    marine_warmth = jnp.einsum(
        "cmzqy,cmzy->cmq",
        skin_warmth_mapping_factors.astype(jnp.float32),
        selected_elements,
        precision=maximal_magnitude,
    ).reshape(lat_count, lon_local)
    driven_tendency = (aloft_state + layer_sensitivity[:, None, None] * marine_warmth[None]).astype(
        jnp.bfloat16
    )
    forced_lat = driven_tendency.transpose(1, 0, 2)

    def one_lat(pair):
        return fourier_rows(pair[0], pair[1], lon_ids, m_local * lax.axis_size("lon"))

    per_lat = lax.map(one_lat, (forced_lat, parallel_nodes))
    wave_sums = lax.psum_scatter(
        per_lat.transpose(1, 0, 2, 3).reshape(
            m_local * lax.axis_size("lon"), lat_count * level_stack * 2
        ),
        "lon",
        scatter_dimension=0,
        tiled=True,
    )
    fourier = wave_sums.reshape(m_local, lat_count, level_stack * 2).astype(jnp.bfloat16)
    degree_local = associated_polynomial_quadrature.shape[2] // lax.axis_size("lat")
    wave_ids = lon_slot * m_local + jnp.arange(m_local, dtype=jnp.int32)
    summed = jnp.einsum(
        "imn,mia->nam",
        associated_polynomial_quadrature,
        fourier,
        preferred_element_type=jnp.float32,
    )
    degree_ids = jnp.arange(degree_local * lax.axis_size("lat"), dtype=jnp.int32)
    spectra = lax.psum_scatter(
        jnp.where(degree_ids[:, None, None] >= wave_ids[None, None, :], summed, 0.0),
        "lat",
        scatter_dimension=0,
        tiled=True,
    )
    wet = water_indicator.astype(jnp.float32)
    sea_flux = jnp.einsum(
        "rckio,rcki->rco",
        heat_transfer_factors.astype(jnp.float32),
        picked_air,
        precision=maximal_magnitude,
    ).reshape(wet.shape)
    top_flag = (lax.axis_index("grp") == 0).astype(jnp.float32)
    heating = FLUX_RATE * sea_flux * wet * top_flag
    warmed = marine_heat.at[0].add(heating)
    stacked = jnp.concatenate([warmed, wet[None]], axis=0)
    extended = with_halo(stacked, (("lat", 1), ("lon", 2)), 2)
    field_ext = extended[:-1]
    wet_ext = extended[-1]
    ocean_out = diffuse(diffuse(field_ext, wet_ext), wet_ext[1:-1, 1:-1])
    return (spectra, ocean_out)


def solution(mesh):
    in_specs = (
        P("grp", "lat", "lon"),
        P("lat"),
        P("grp"),
        P("grp"),
        P("lat", "lon", None),
        P("grp", "lat", "lon"),
        P("lat", "lon"),
        P("lat", "lon", None),
        P("lat", "lon", None, None, None),
        P("lat", "lon", None),
        P("lat", "lon", None, None, None),
    )
    out_specs = (P("lat", "grp", "lon"), P("grp", "lat", "lon"))
    return jax.shard_map(
        per_device, mesh=mesh, in_specs=in_specs, out_specs=out_specs, check_vma=False
    )
```

profile of v0, /device:TPU:6, one launch (start us, length us, event | category | flops | bytes accessed | tf_op | source)
XLA Modules:
  0.0 495.9 jit_solution(15107213000646228801)
XLA Ops:
  7.2 1.0 copy.78
  8.2 0.8 fusion.44
  9.0 14.4 %all-reduce = (bf16[8,324]{1,0:T(8,128)(2,1)S(1)}, f32[32,128]{1,0:T(8,128)S(1)}) all-reduce(f32[8,324]{1,0:T(8,128)S(1)} %fusion.44, f32[32,128]{1,0:T(8,128)S(1)} %select_bitcast_fusion.1), channel_id=1, replica_groups=mesh['grp'=4,'lat'=16,'lon'=8] {'grp'}, use_global_device_ids=true, to_apply=%region_6.7 | all-reduce | flops 6688 | bytes 48320 | tf_op jit(solution)/shard_map/psum | solution.py:83
  23.4 28.2 %all_gather.12 = f32[32,1024]{1,0:T(8,128)} all-gather(f32[32,128]{1,0:T(8,128)S(1)} %get-tuple-element.81), channel_id=1, replica_groups=mesh['grp'=4,'lat'=16,'lon'=8] {'lon'}, dimensions={1}, use_global_device_ids=true | all-gather | bytes 147456 | tf_op jit(solution)/shard_map/all_gather | solution.py:92
  51.6 0.9 copy.45
  52.5 0.7 compare_and_fusion
  53.8 76.0 %all-gather.3.cloned.1.call-done = f32[512,1024]{1,0:T(8,128)} async-done(((f32[32,1024]{1,0:T(8,128)}), f32[512,1024]{1,0:T(8,128)}) %all-gather.3.cloned.1.call-update) | async-done | bytes 2097168 | tf_op jit(solution)/shard_map/all_gather | solution.py:93
  129.8 2.7 reshape.211
  132.5 3.5 gather_fusion
  136.0 0.6 broadcast_select_fusion
  136.6 3.1 fusion.18
  140.0 122.4 %while.12 = (s32[]{:T(128)}, f32[8,640,2,2]{1,3,2,0:T(2,128)S(1)}, bf16[8,2,324]{2,1,0:T(2,128)(2,1)S(1)}, s32[8]{0:T(128)S(1)}, s32[]{:T(128)}, /*index=5*/s32[]{:T(128)}, f32[]{:T(128)}, s32[]{:T(128)}) while((s32[]{:T(128)}, f32[8,640,2,2]{1,3,2,0:T(2,128)S(1)}, bf16[8,2,324]{2,1,0:T(2,128)(2,1)S(1)}, s32[8]{0:T(128)S(1)}, ...), condition=%wide.region_2.3_spmd.clone, body=%wide.region_1.0_spmd.clone.sunk | while | flops 6640339 | bytes 1726569 | solution.py:113
  140.2 0.6 dynamic_slice.17
  143.1 0.6 multiply_compare_fusion.2
  143.7 11.5 %fusion.58 = (bf16[324,640]{1,0:T(8,128)(2,1)S(1)}, bf16[324,640]{1,0:T(8,128)(2,1)S(1)}) fusion(f32[]{:T(128)S(6)} %div.19, s32[]{:T(128)S(6)} %select_n.127, s32[324]{0:T(512)S(1)} %iota_add_fusion.4, pred[]{:T(512)S(6)} %lt.152, pred[640]{0:T(1024)(128)(4,1)S(1)} %multiply_compare_fusion.2, pred[324]{0:T(512)(128)(4,1)S(1)} %broadcast_compare_fusion.2), kind=kLoop, calls=%fused_computation.7.clone.1 | loop fusion | flops 3317760 | bytes 831709 | tf_op jit(solution)/shard_map/while/body/eval_jaxpr/convert_element_type | solution.py:34
  155.4 0.6 dynamic_slice.17
  157.8 0.6 broadcast_compare_fusion.2
  158.3 0.6 multiply_compare_fusion.2
  158.9 11.5 %fusion.58 = (bf16[324,640]{1,0:T(8,128)(2,1)S(1)}, bf16[324,640]{1,0:T(8,128)(2,1)S(1)}) fusion(f32[]{:T(128)S(6)} %div.19, s32[]{:T(128)S(6)} %select_n.127, s32[324]{0:T(512)S(1)} %iota_add_fusion.4, pred[]{:T(512)S(6)} %lt.152, pred[640]{0:T(1024)(128)(4,1)S(1)} %multiply_compare_fusion.2, pred[324]{0:T(512)(128)(4,1)S(1)} %broadcast_compare_fusion.2), kind=kLoop, calls=%fused_computation.7.clone.1 | loop fusion | flops 3317760 | bytes 831709 | tf_op jit(solution)/shard_map/while/body/eval_jaxpr/convert_element_type | solution.py:34
  170.7 0.6 dynamic_slice.17
  173.0 0.6 broadcast_compare_fusion.2
  173.6 0.6 multiply_compare_fusion.2
  174.2 11.5 %fusion.58 = (bf16[324,640]{1,0:T(8,128)(2,1)S(1)}, bf16[324,640]{1,0:T(8,128)(2,1)S(1)}) fusion(f32[]{:T(128)S(6)} %div.19, s32[]{:T(128)S(6)} %select_n.127, s32[324]{0:T(512)S(1)} %iota_add_fusion.4, pred[]{:T(512)S(6)} %lt.152, pred[640]{0:T(1024)(128)(4,1)S(1)} %multiply_compare_fusion.2, pred[324]{0:T(512)(128)(4,1)S(1)} %broadcast_compare_fusion.2), kind=kLoop, calls=%fused_computation.7.clone.1 | loop fusion | flops 3317760 | bytes 831709 | tf_op jit(solution)/shard_map/while/body/eval_jaxpr/convert_element_type | solution.py:34
  186.0 0.6 dynamic_slice.17
  188.3 0.6 broadcast_compare_fusion.2
  188.9 0.6 multiply_compare_fusion.2
  189.4 11.5 %fusion.58 = (bf16[324,640]{1,0:T(8,128)(2,1)S(1)}, bf16[324,640]{1,0:T(8,128)(2,1)S(1)}) fusion(f32[]{:T(128)S(6)} %div.19, s32[]{:T(128)S(6)} %select_n.127, s32[324]{0:T(512)S(1)} %iota_add_fusion.4, pred[]{:T(512)S(6)} %lt.152, pred[640]{0:T(1024)(128)(4,1)S(1)} %multiply_compare_fusion.2, pred[324]{0:T(512)(128)(4,1)S(1)} %broadcast_compare_fusion.2), kind=kLoop, calls=%fused_computation.7.clone.1 | loop fusion | flops 3317760 | bytes 831709 | tf_op jit(solution)/shard_map/while/body/eval_jaxpr/convert_element_type | solution.py:34
  201.2 0.6 dynamic_slice.17
  203.5 0.6 broadcast_compare_fusion.2
  204.1 0.6 multiply_compare_fusion.2
  204.7 11.5 %fusion.58 = (bf16[324,640]{1,0:T(8,128)(2,1)S(1)}, bf16[324,640]{1,0:T(8,128)(2,1)S(1)}) fusion(f32[]{:T(128)S(6)} %div.19, s32[]{:T(128)S(6)} %select_n.127, s32[324]{0:T(512)S(1)} %iota_add_fusion.4, pred[]{:T(512)S(6)} %lt.152, pred[640]{0:T(1024)(128)(4,1)S(1)} %multiply_compare_fusion.2, pred[324]{0:T(512)(128)(4,1)S(1)} %broadcast_compare_fusion.2), kind=kLoop, calls=%fused_computation.7.clone.1 | loop fusion | flops 3317760 | bytes 831709 | tf_op jit(solution)/shard_map/while/body/eval_jaxpr/convert_element_type | solution.py:34
  216.5 0.6 dynamic_slice.17
  218.8 0.6 broadcast_compare_fusion.2
  219.4 0.6 multiply_compare_fusion.2
  219.9 11.5 %fusion.58 = (bf16[324,640]{1,0:T(8,128)(2,1)S(1)}, bf16[324,640]{1,0:T(8,128)(2,1)S(1)}) fusion(f32[]{:T(128)S(6)} %div.19, s32[]{:T(128)S(6)} %select_n.127, s32[324]{0:T(512)S(1)} %iota_add_fusion.4, pred[]{:T(512)S(6)} %lt.152, pred[640]{0:T(1024)(128)(4,1)S(1)} %multiply_compare_fusion.2, pred[324]{0:T(512)(128)(4,1)S(1)} %broadcast_compare_fusion.2), kind=kLoop, calls=%fused_computation.7.clone.1 | loop fusion | flops 3317760 | bytes 831709 | tf_op jit(solution)/shard_map/while/body/eval_jaxpr/convert_element_type | solution.py:34
  231.7 0.6 dynamic_slice.17
  234.0 0.6 broadcast_compare_fusion.2
  235.2 11.5 %fusion.58 = (bf16[324,640]{1,0:T(8,128)(2,1)S(1)}, bf16[324,640]{1,0:T(8,128)(2,1)S(1)}) fusion(f32[]{:T(128)S(6)} %div.19, s32[]{:T(128)S(6)} %select_n.127, s32[324]{0:T(512)S(1)} %iota_add_fusion.4, pred[]{:T(512)S(6)} %lt.152, pred[640]{0:T(1024)(128)(4,1)S(1)} %multiply_compare_fusion.2, pred[324]{0:T(512)(128)(4,1)S(1)} %broadcast_compare_fusion.2), kind=kLoop, calls=%fused_computation.7.clone.1 | loop fusion | flops 3317760 | bytes 831709 | tf_op jit(solution)/shard_map/while/body/eval_jaxpr/convert_element_type | solution.py:34
  247.0 0.6 dynamic_slice.17
  249.3 0.6 broadcast_compare_fusion.2
  249.9 0.6 multiply_compare_fusion.2
  250.5 11.5 %fusion.58 = (bf16[324,640]{1,0:T(8,128)(2,1)S(1)}, bf16[324,640]{1,0:T(8,128)(2,1)S(1)}) fusion(f32[]{:T(128)S(6)} %div.19, s32[]{:T(128)S(6)} %select_n.127, s32[324]{0:T(512)S(1)} %iota_add_fusion.4, pred[]{:T(512)S(6)} %lt.152, pred[640]{0:T(1024)(128)(4,1)S(1)} %multiply_compare_fusion.2, pred[324]{0:T(512)(128)(4,1)S(1)} %broadcast_compare_fusion.2), kind=kLoop, calls=%fused_computation.7.clone.1 | loop fusion | flops 3317760 | bytes 831709 | tf_op jit(solution)/shard_map/while/body/eval_jaxpr/convert_element_type | solution.py:34
  262.5 0.9 copy.58
  263.5 37.5 %reduce-scatter.7.cloned.1.call-done = f32[80,32]{1,0:T(8,128)} async-done(((f32[640,32]{1,0:T(8,128)}), f32[80,32]{1,0:T(8,128)}) %reduce-scatter.7.cloned.1.call-update) | async-done | bytes 10256
  301.1 0.8 copy.59
  302.1 0.9 fusion.17
  303.0 24.5 %copy.60 = f32[1280,4,80]{1,2,0:T(8,128)} copy(f32[1280,4,80]{0,1,2:T(4,128)S(1)} %fusion.17) | data formatting | bytes 3276800
  327.5 33.2 %reshape.248 = f32[1280,320]{1,0:T(8,128)} reshape(f32[1280,80,4]{2,1,0:T(8,128)} %bitcast.72) | data formatting | bytes 3276800
  360.8 0.7 copy-done.4
  361.7 24.7 %all-gather = bf16[8,324,8]{1,2,0:T(8,128)(2,1)S(1)} all-gather(bf16[1,324,8]{1,2,0:T(8,128)(2,1)S(1)} %select_bitcast_fusion.2), channel_id=1, replica_groups=mesh['grp'=4,'lat'=16,'lon'=8] {'lon'}, dimensions={0}, use_global_device_ids=true | all-gather | bytes 46656 | tf_op jit(solution)/shard_map/all_gather | solution.py:84
  386.6 46.6 %all_gather.15 = bf16[128,2592]{1,0:T(8,128)(2,1)S(1)} all-gather(bf16[8,2592]{1,0:T(8,128)(2,1)S(1)} %bitcast.78), channel_id=1, replica_groups=mesh['grp'=4,'lat'=16,'lon'=8] {'lat'}, dimensions={0}, use_global_device_ids=true | all-gather | bytes 705024 | tf_op jit(solution)/shard_map/all_gather | solution.py:85
  433.2 17.2 %reshape.221 = f32[55296,6]{1,0:T(8,128)} reshape(bf16[128,2592]{1,0:T(8,128)(2,1)S(1)} %all_gather.15) | data formatting | bytes 1990656 | tf_op jit(solution)/shard_map/reshape | solution.py:89
  450.4 9.7 %gather_fusion.1 = f32[128,6]{1,0:T(8,128)S(1)} fusion(f32[55296,6]{1,0:T(8,128)} %reshape.221, s32[1024]{0:T(1024)S(1)} %pad_clamp_fusion), kind=kCustom, calls=%fused_computation.1 | custom fusion | bytes 6656 | tf_op jit(solution)/shard_map/jit(_take)/gather | solution.py:88
  460.5 0.7 fusion.21
  461.3 2.5 collective-permute-start
  463.8 3.3 collective-permute-start.1
  467.2 3.0 collective-permute-done.1
  470.3 3.9 collective-permute-start.2
  474.2 1.3 collective-permute-start.3
  475.5 0.9 collective-permute-done.2
  476.5 4.3 collective-permute-done.3
  481.5 0.8 fusion.37
  482.3 3.8 reshape.249
  486.1 3.2 copy.52
  (93 shorter events, 6.3 us)
Async XLA Ops:
  7.2 294.9 %copy-start = (bf16[8,80,1280]{2,1,0:T(8,128)(2,1)S(1)}, bf16[8,80,1280]{2,1,0:T(8,128)(2,1)}, u32[]{:S(2)}) copy-start(bf16[8,80,1280]{2,1,0:T(8,128)(2,1)} %param.19) | copy-start | bytes 4915204
  7.2 122.6 %all-gather.3.cloned.1.call-start = ((), (), s32[]{:S(2)}) async-start(), calls=%async_computation.2 | async-start | bytes 2228224 | tf_op jit(solution)/shard_map/all_gather | solution.py:93
  51.6 249.5 %reduce-scatter.7.cloned.1.call-start = ((), (), s32[]{:S(2)}) async-start(), calls=%async_computation.3 | async-start | bytes 368640
  136.6 3.3 copy-start.3
  136.6 3.3 copy-start.5
  136.6 3.4 copy-start.6
  263.4 218.9 %reduce-scatter.9.cloned.1.call-start = ((), (), s32[]{:S(2)}) async-start(), calls=%async_computation.4 | async-start | bytes 2088960
  360.8 0.7 copy-start.4
  433.2 27.3 %copy-start.2 = (s32[32,128]{1,0:T(8,128)S(1)}, s32[32,128]{1,0:T(8,128)}, u32[]{:S(2)}) copy-start(s32[32,128]{1,0:T(8,128)} %param.21) | copy-start | bytes 49156
  433.2 27.3 %copy-start.7 = (bf16[32,1,4,6,128]{4,2,3,1,0:T(4,128)(2,1)S(1)}, bf16[32,1,4,6,128]{4,2,3,1,0:T(4,128)(2,1)}, u32[]{:S(2)}) copy-start(bf16[32,1,4,6,128]{4,2,3,1,0:T(4,128)(2,1)} %param.23) | copy-start | bytes 589828
  461.3 5.9 %collective-permute-start = (f32[5,2,128]{2,1,0:T(2,128)S(1)}, f32[5,2,128]{2,1,0:T(2,128)S(1)}, u32[]{:S(2)}, u32[]{:S(2)}) collective-permute-start(f32[5,2,128]{2,1,0:T(2,128)S(1)} %get-tuple-element.86), channel_id=1, source_target_pairs={{0,8},{8,16},{16,24},{24,32},{32,40},{40,48},{48,56},{56,64},{64,7... | collective-permute-start | bytes 15368 | tf_op jit(solution)/shard_map/ppermute | solution.py:21
  463.8 6.4 %collective-permute-start.1 = (f32[5,2,128]{2,1,0:T(2,128)S(1)}, f32[5,2,128]{2,1,0:T(2,128)S(1)}, u32[]{:S(2)}, u32[]{:S(2)}) collective-permute-start(f32[5,2,128]{2,1,0:T(2,128)S(1)} %get-tuple-element.87), channel_id=1, source_target_pairs={{8,0},{16,8},{24,16},{32,24},{40,32},{48,40},{56,48},{64,56},{72,6... | collective-permute-start | bytes 15368 | tf_op jit(solution)/shard_map/ppermute | solution.py:24
  470.3 6.1 %collective-permute-start.2 = (f32[5,36,2]{2,1,0:T(8,128)S(1)}, f32[5,36,2]{2,1,0:T(8,128)S(1)}, u32[]{:S(2)}, u32[]{:S(2)}) collective-permute-start(f32[5,36,2]{2,1,0:T(8,128)S(1)} %get-tuple-element.84), channel_id=1, source_target_pairs={{0,1},{1,2},{2,3},{3,4},{4,5},{5,6},{6,7},{8,9},{9,10},{10,11},{11... | collective-permute-start | bytes 4328 | tf_op jit(solution)/shard_map/ppermute | solution.py:21
  474.2 6.6 %collective-permute-start.3 = (f32[5,36,2]{2,1,0:T(8,128)S(1)}, f32[5,36,2]{2,1,0:T(8,128)S(1)}, u32[]{:S(2)}, u32[]{:S(2)}) collective-permute-start(f32[5,36,2]{2,1,0:T(8,128)S(1)} %get-tuple-element.85), channel_id=1, source_target_pairs={{1,0},{2,1},{3,2},{4,3},{5,4},{6,5},{7,6},{9,8},{10,9},{11,10},{12... | collective-permute-start | bytes 4328 | tf_op jit(solution)/shard_map/ppermute | solution.py:24
  486.1 3.2 copy-start.1
Sparse Core Ops, SparseCore 0:
  51.7 78.0 all-gather.2
  263.5 37.4 reduce-scatter.6
  360.9 80.3 reduce-scatter.8
where the time goes:
time: 499 us; the launch traced here: 496 us
  waiting for transfers between devices  122 us (24%)
  blocking collectives  114 us (23%)
  local copies, waits for them, and re-layouts  109 us (22%)
  other arithmetic  105 us (21%)
  loops' own time  14.7 us (3%)
  between operations  14.1 us (3%)
  starting transfers between devices  11.1 us (2%)
  matrix products  6.58 us (1%)
    convert_element_type x8, other arithmetic, fourier_rows(): cosine = jnp.where(usable, jnp.cos(angles), 0.0).astype(jnp.bfloat16)  91.8 us
    all_gather x1, waiting for transfers between devices, per_device(): entire_ocean_field = lax.all_gather(band_sea, 'lat', axis=0, tiled=True)  76 us
    unnamed x26, local copies, waits for them, and re-layouts  69.1 us
    all_gather x1, blocking collectives, per_device(): lax.all_gather(band_flux.astype(jnp.bfloat16), 'lat', axis=0, tiled=True)  46.6 us
    unnamed x5, waiting for transfers between devices  37.6 us
    all_gather x1, blocking collectives, per_device(): band_sea = lax.all_gather(sea_top, 'lon', axis=1, tiled=True)  28.2 us
    all_gather x1, blocking collectives, per_device(): band_flux = lax.all_gather(column_flux, 'lon', axis=1, tiled=True)  24.7 us
    reshape x1, local copies, waits for them, and re-layouts, per_device(): whole_flux.reshape(-1, block_air)  17.2 us
  transfers between devices with their start and end apart: 7, of which 5 were waited for; matrix products, arithmetic and copies ran while one was open for 6% of the time, Pallas kernels for 0%

commit v1 on v0

v1 whole, which is shorter than its diff:
```python
import functools
import math

import jax
import jax.numpy as jnp
from jax import lax
from jax.experimental import pallas as pl
from jax.experimental.pallas import tpu as pltpu
from jax.sharding import PartitionSpec as P

TWO_PI = 6.283185307179586
FLUX_RATE = 0.5
KAPPA = 0.2
MESH_ID = pl.DeviceIdType.MESH
LANES = 128
PACK = 21
BLK_PAD = 64
VMEM_LIMIT = 48 * 1024 * 1024


def shifted(index, offset, count):
    return lax.rem(index + offset, count)


def greet(partners):
    barrier = pltpu.get_barrier_semaphore()
    for partner in partners:
        pl.semaphore_signal(barrier, inc=1, device_id=partner, device_id_type=MESH_ID)
    pl.semaphore_wait(barrier, len(partners))


def remote(src, dst, send_sem, recv_sem, partner):
    return pltpu.make_async_remote_copy(
        src_ref=src,
        dst_ref=dst,
        send_sem=send_sem,
        recv_sem=recv_sem,
        device_id=partner,
        device_id_type=MESH_ID,
    )


def landed(ref, sem):
    pltpu.make_async_copy(ref, ref, sem).wait()


def turn(phase, count, inverse):
    rest = phase - jnp.floor(phase * inverse + 0.5) * count
    part = rest * inverse
    square = part * part
    cosine = jnp.zeros_like(part)
    sine = jnp.zeros_like(part)
    for power in range(8, -1, -1):
        sign = -1.0 if power % 2 else 1.0
        cosine = cosine * square + sign * TWO_PI ** (2 * power) / math.factorial(2 * power)
        sine = sine * square - sign * TWO_PI ** (2 * power + 1) / math.factorial(2 * power + 1)
    return cosine, sine * part


def spread_kernel(
    sizes,
    nodes_ref,
    inverse_ref,
    partial_ref,
    heat_ref,
    sea_ref,
    flux_ref,
    e1_ref,
    e2_ref,
    stage,
    part,
    gathered,
    sea0_send,
    sea0_recv,
    flux0_send,
    flux0_recv,
    sea1_send,
    sea1_recv,
    flux1_send,
    flux1_recv,
    sea2_send,
    sea2_recv,
    flux2_send,
    flux2_recv,
):
    grps, lats, lons, lat_count, lon_local, m_local, block_air = sizes
    g, t, y = (lax.axis_index(name) for name in ("grp", "lat", "lon"))
    lon_per, lat_per = lons // grps, lats // grps
    sea_owner, yy = y // lon_per, lax.rem(y, lon_per)
    flux_owner, tt = t // lat_per, lax.rem(t, lat_per)

    def tables(i):
        count = nodes_ref[i].astype(jnp.float32)
        inverse = inverse_ref[i]
        wide = lons * LANES
        lane = lax.broadcasted_iota(jnp.int32, (8, wide), 1)
        row = lax.broadcasted_iota(jnp.int32, (8, wide), 0)
        inner = lane % LANES
        wave = (lane // LANES) * m_local + inner
        start = y * lon_local
        wave_f = wave.astype(jnp.float32)
        row_f = row.astype(jnp.float32)
        base_f = start.astype(jnp.float32)
        high = turn((base_f + 8 * block_air * row_f) * wave_f, count, inverse)
        low = turn((block_air * row_f) * wave_f, count, inverse)
        slot = turn(row_f * wave_f, count, inverse)
        usable = (inner < m_local) & (2.0 * wave_f < count)
        e2_ref[pl.ds(pl.multiple_of(i * 8, 8), 8), :wide] = jnp.where(usable, slot[0], 0.0)
        e2_ref[pl.ds(pl.multiple_of(i * 8, 8), 8), wide:] = jnp.where(usable, slot[1], 0.0)
        for pair in range(BLK_PAD // 16):
            real, imag = [], []
            for b in (2 * pair, 2 * pair + 1):
                hr, hi = high[0][b : b + 1], high[1][b : b + 1]
                real.append(hr * low[0] - hi * low[1])
                imag.append(hr * low[1] + hi * low[0])
            where = pl.ds(pl.multiple_of(i * BLK_PAD + pair * 16, 16), 16)
            e1_ref[where, :wide] = jnp.concatenate(real, axis=0).astype(jnp.bfloat16)
            e1_ref[where, wide:] = jnp.concatenate(imag, axis=0).astype(jnp.bfloat16)

    def some_tables(low, high):
        lax.fori_loop(low, high, lambda i, c: (tables(i), c)[1], 0)

    rows3 = 3 * lat_count
    lane = lax.broadcasted_iota(jnp.int32, (lat_count, LANES), 1)
    span = PACK * block_air
    for c in range(3):
        whole = partial_ref[...]
        moved = whole if c == 0 else pltpu.roll(whole, 3 * LANES - c * span, 1)
        limit = min(span, lon_local - c * span)
        part[c * lat_count : (c + 1) * lat_count, :] = jnp.where(
            lane < limit, moved[:, :LANES], 0.0
        )
    stage[...] = heat_ref[0].astype(jnp.bfloat16)

    greet(
        [{"grp": shifted(g, d, grps)} for d in range(1, grps)]
        + [{"lon": shifted(y, d, lons)} for d in range(1, lons)]
        + [{"lat": shifted(t, d, lats)} for d in range(1, lats)]
    )

    sea0 = remote(stage, sea_ref.at[t, yy], sea0_send, sea0_recv, {"grp": sea_owner})
    flux0 = remote(
        part, gathered.at[g], flux0_send, flux0_recv.at[g], {"grp": flux_owner}
    )

    @pl.when((g == 0) & (sea_owner != 0))
    def _():
        sea0.start()

    @pl.when((g == 0) & (sea_owner == 0))
    def _():
        sea_ref[t, yy] = stage[...]

    @pl.when(g != flux_owner)
    def _():
        flux0.start()

    some_tables(0, 2)

    @pl.when((g == sea_owner) & (sea_owner != 0))
    def _():
        landed(sea_ref.at[t, yy], sea0_recv)

    @pl.when(g == sea_owner)
    def _():
        for d in range(1, lons):
            remote(
                sea_ref.at[t, yy],
                sea_ref.at[t, yy],
                sea1_send.at[d],
                sea1_recv.at[yy],
                {"lon": shifted(y, d, lons)},
            ).start()

    @pl.when(g == flux_owner)
    def _():
        gathered[g] = part[...]
        for d in range(1, grps):
            other = shifted(g, d, grps)
            landed(gathered.at[other], flux0_recv.at[other])
        total = gathered[0]
        for other in range(1, grps):
            total = total + gathered[other]
        flux_ref[y, tt] = jnp.concatenate(
            [total, jnp.zeros((32 - rows3, LANES), jnp.float32)], axis=0
        ).astype(jnp.bfloat16)
        for d in range(1, lats):
            remote(
                flux_ref.at[y, tt],
                flux_ref.at[y, tt],
                flux1_send.at[d],
                flux1_recv.at[tt],
                {"lat": shifted(t, d, lats)},
            ).start()

    some_tables(2, 4)

    for k in range(lon_per):
        @pl.when(g * lon_per + k != y)
        def _():
            landed(sea_ref.at[t, k], sea1_recv.at[k])

    for d in range(1, lats):
        remote(
            sea_ref.at[t],
            sea_ref.at[t],
            sea2_send.at[d],
            sea2_recv.at[t],
            {"lat": shifted(t, d, lats)},
        ).start()

    for k in range(lat_per):
        @pl.when(g * lat_per + k != t)
        def _():
            landed(flux_ref.at[y, k], flux1_recv.at[k])

    for d in range(1, lons):
        remote(
            flux_ref.at[y],
            flux_ref.at[y],
            flux2_send.at[d],
            flux2_recv.at[y],
            {"lon": shifted(y, d, lons)},
        ).start()

    some_tables(4, lat_count)

    for d in range(1, lons):
        other = shifted(y, d, lons)
        landed(flux_ref.at[other], flux2_recv.at[other])
    for d in range(1, lats):
        other = shifted(t, d, lats)
        landed(sea_ref.at[other], sea2_recv.at[other])

    @pl.when((g == 0) & (sea_owner != 0))
    def _():
        landed(stage, sea0_send)

    @pl.when(g != flux_owner)
    def _():
        landed(part, flux0_send)

    @pl.when(g == sea_owner)
    def _():
        for d in range(1, lons):
            landed(sea_ref.at[t, yy], sea1_send.at[d])

    @pl.when(g == flux_owner)
    def _():
        for d in range(1, lats):
            landed(flux_ref.at[y, tt], flux1_send.at[d])

    for d in range(1, lats):
        landed(sea_ref.at[t], sea2_send.at[d])
    for d in range(1, lons):
        landed(flux_ref.at[y], flux2_send.at[d])


def spectral_kernel(
    sizes,
    sens_ref,
    inverse_ref,
    warmth_ref,
    flux_ref,
    aloft_ref,
    mask_ref,
    e1_ref,
    e2_ref,
    quad_ref,
    heat_ref,
    water_ref,
    spec_ref,
    ocean_ref,
    warmth_in,
    flux_in,
    ext,
    waves,
    waves_in,
    spread,
    sums,
    turned,
    turned_in,
    warmth_send,
    warmth_recv,
    flux_send,
    flux_recv,
    halo_send,
    halo_recv,
    waves_send,
    waves_recv,
    turned_send,
    turned_recv,
):
    grps, lats, lons, lat_count, levels, m_local, degrees, olev, rows, cols = sizes
    g, t, y = (lax.axis_index(name) for name in ("grp", "lat", "lon"))
    wide = lons * LANES
    parts = 2 * levels
    n_local = degrees // lats
    north, south = shifted(t, lats - 1, lats), shifted(t, 1, lats)
    west, east = shifted(y, lons - 1, lons), shifted(y, 1, lons)
    mid_rows, mid_cols = slice(8, 8 + rows), slice(LANES, LANES + cols)
    first_rows, last_rows = slice(8, 16), slice(rows, rows + 8)
    low_rows, high_rows = slice(0, 8), slice(8 + rows, 16 + rows)
    low_cols, high_cols = slice(0, LANES), slice(LANES + cols, 2 * LANES + cols)
    halo = [
        ({"lat": south}, last_rows, low_rows, mid_cols),
        ({"lat": north}, first_rows, high_rows, mid_cols),
        ({"lon": east}, mid_rows, mid_rows, low_cols),
        ({"lon": west}, mid_rows, mid_rows, high_cols),
        ({"lat": south, "lon": east}, last_rows, low_rows, low_cols),
        ({"lat": south, "lon": west}, last_rows, low_rows, high_cols),
        ({"lat": north, "lon": east}, first_rows, high_rows, low_cols),
        ({"lat": north, "lon": west}, first_rows, high_rows, high_cols),
    ]

    for level in range(olev):
        ext[level, mid_rows, mid_cols] = heat_ref[level]
    wet_mid = water_ref[...].astype(jnp.float32)
    ext[olev, mid_rows, mid_cols] = wet_mid

    greet(
        [{"grp": shifted(g, d, grps)} for d in range(1, grps)]
        + [{"lon": shifted(y, d, lons)} for d in range(1, lons)]
        + [{"lat": shifted(t, d, lats)} for d in range(1, lats)]
        + [partner for partner, _, _, _ in halo[4:]]
    )

    flux_copy = remote(
        flux_ref, flux_in.at[g], flux_send, flux_recv.at[g], {"grp": jnp.int32(0)}
    )

    @pl.when(g != 0)
    def _():
        flux_copy.start()

    for d in range(1, grps):
        remote(
            warmth_ref,
            warmth_in.at[g],
            warmth_send.at[d],
            warmth_recv.at[g],
            {"grp": shifted(g, d, grps)},
        ).start()

    @pl.when(g == 0)
    def _():
        total = flux_ref[...]
        for other in range(1, grps):
            landed(flux_in.at[other], flux_recv.at[other])
            total = total + flux_in[other]
        ext[0, mid_rows, mid_cols] = heat_ref[0] + FLUX_RATE * total * wet_mid

    for index, (partner, src_rows, dst_rows, dst_cols) in enumerate(halo):
        remote(
            ext.at[:, src_rows, mid_cols],
            ext.at[:, dst_rows, dst_cols],
            halo_send.at[index],
            halo_recv.at[index],
            partner,
        ).start()

    warmth_in[g] = warmth_ref[...]
    for d in range(1, grps):
        other = shifted(g, d, grps)
        landed(warmth_in.at[other], warmth_recv.at[other])
    warmth = warmth_in[0]
    for other in range(1, grps):
        warmth = warmth + warmth_in[other]
    warmth = warmth * mask_ref[...]
    forced = jnp.concatenate(
        [aloft_ref[8 * l : 8 * l + 8, :] + sens_ref[l] * warmth for l in range(levels)], axis=0
    )
    lane = lax.broadcasted_iota(jnp.int32, forced.shape, 1)
    blocks = jnp.concatenate(
        [jnp.where(lane // BLK_PAD == i, forced, 0.0) for i in range(lat_count)], axis=0
    ).astype(jnp.bfloat16)
    real = jnp.dot(blocks, e1_ref[:, :wide], preferred_element_type=jnp.float32)
    imag = jnp.dot(blocks, e1_ref[:, wide:], preferred_element_type=jnp.float32)
    for i in range(lat_count):
        slot_r = e2_ref[8 * i : 8 * i + 8, :wide] * inverse_ref[i]
        slot_i = e2_ref[8 * i : 8 * i + 8, wide:] * inverse_ref[i]
        for l in range(levels):
            at = (i * levels + l) * 8
            re, im = real[at : at + 8], imag[at : at + 8]
            out_r = jnp.sum(re * slot_r - im * slot_i, axis=0, keepdims=True)
            out_i = jnp.sum(re * slot_i + im * slot_r, axis=0, keepdims=True)
            for c, out in enumerate((out_r, out_i)):
                row = (2 * l + c) * lat_count + i
                for k in range(lons):
                    waves[k, row : row + 1, :] = out[:, k * LANES : (k + 1) * LANES]

    for d in range(1, lons):
        other = shifted(y, d, lons)
        remote(
            waves.at[other], waves_in.at[y], waves_send.at[d], waves_recv.at[y], {"lon": other}
        ).start()

    for index, (partner, src_rows, dst_rows, dst_cols) in enumerate(halo):
        landed(ext.at[:, dst_rows, dst_cols], halo_recv.at[index])
    shape = (rows + 16, cols + 2 * LANES)
    row_id = lax.broadcasted_iota(jnp.int32, shape, 0) + (t * rows - 8)
    col_id = lax.broadcasted_iota(jnp.int32, shape, 1) + (y * cols - LANES)
    inside = (row_id >= 0) & (row_id < rows * lats) & (col_id >= 0) & (col_id < cols * lons)
    wet = jnp.where(inside, ext[olev], 0.0)
    moves = ((1, 0), (shape[0] - 1, 0), (1, 1), (shape[1] - 1, 1))
    wet_near = [pltpu.roll(wet, shift, axis) for shift, axis in moves]
    for level in range(olev):
        field = ext[level]
        for _ in range(2):
            total = jnp.zeros_like(field)
            for (shift, axis), near in zip(moves, wet_near):
                total = total + near * (pltpu.roll(field, shift, axis) - field)
            field = field + KAPPA * wet * total
        ocean_ref[level] = field[mid_rows, mid_cols]

    waves_in[y] = waves[y]
    for d in range(1, lons):
        other = shifted(y, d, lons)
        landed(waves_in.at[other], waves_recv.at[other])
    total = waves_in[0]
    for other in range(1, lons):
        total = total + waves_in[other]
    total = total.astype(jnp.bfloat16).astype(jnp.float32)
    rest = jnp.zeros((LANES - parts * lat_count, LANES), jnp.float32)
    columns = jnp.transpose(jnp.concatenate([total, rest], axis=0))
    for j in range(parts * lat_count):
        spread[j] = jnp.broadcast_to(columns[:m_local, j : j + 1], (m_local, LANES))

    sums[...] = jnp.zeros_like(sums)

    def chunk(c, carry):
        lanes = pl.ds(pl.multiple_of(c * LANES, LANES), LANES)

        def some_waves(b, inner):
            own = pl.ds(pl.multiple_of(b * 16, 16), 16)
            acc = [jnp.zeros((16, LANES), jnp.float32) for _ in range(parts)]
            for i in range(lat_count):
                quad = quad_ref[i, own, lanes].astype(jnp.float32)
                for a in range(parts):
                    acc[a] = acc[a] + quad * spread[a * lat_count + i, own, :]
            for a in range(parts):
                sums[pl.ds(pl.multiple_of(a * m_local + b * 16, 16), 16), :] = acc[a]
            return inner

        lax.fori_loop(0, m_local // 16, some_waves, 0)
        turned[pl.ds(pl.multiple_of(c * LANES, LANES), LANES), :] = jnp.transpose(
            sums[...]
        ).astype(jnp.bfloat16)
        return carry

    lax.fori_loop(0, degrees // LANES, chunk, 0)

    def block(k):
        return turned.at[pl.ds(pl.multiple_of(k * n_local, 16), n_local), :]

    for d in range(1, lats):
        other = shifted(t, d, lats)
        remote(
            block(other), turned_in.at[t], turned_send.at[d], turned_recv.at[t], {"lat": other}
        ).start()
    result = turned[pl.ds(pl.multiple_of(t * n_local, 16), n_local), :].astype(jnp.float32)
    for d in range(1, lats):
        other = shifted(t, lats - d, lats)
        landed(turned_in.at[other], turned_recv.at[other])
        result = result + turned_in[other].astype(jnp.float32)
    lane = lax.broadcasted_iota(jnp.int32, result.shape, 1)
    degree = lax.broadcasted_iota(jnp.int32, result.shape, 0) + t * n_local
    spec_ref[...] = jnp.where(degree >= lane % m_local + y * m_local, result, 0.0)

    @pl.when(g != 0)
    def _():
        landed(flux_ref, flux_send)

    for d in range(1, grps):
        landed(warmth_ref, warmth_send.at[d])
    for index, (partner, src_rows, dst_rows, dst_cols) in enumerate(halo):
        landed(ext.at[:, src_rows, mid_cols], halo_send.at[index])
    for d in range(1, lons):
        landed(waves.at[0], waves_send.at[d])
    for d in range(1, lats):
        landed(turned_in.at[0], turned_send.at[d])


def per_device(
    aloft_gridpoint,
    parallel_nodes,
    layer_pressure_share,
    layer_sensitivity,
    associated_polynomial_quadrature,
    marine_heat,
    water_indicator,
    heat_feeding_panels,
    heat_transfer_factors,
    skin_warmth_feeding_panels,
    skin_warmth_mapping_factors,
):
    grps, lats, lons = (lax.axis_size(name) for name in ("grp", "lat", "lon"))
    g, y = lax.axis_index("grp"), lax.axis_index("lon")
    levels, lat_count, lon_local = aloft_gridpoint.shape
    block_air = heat_transfer_factors.shape[3]
    blocks = lon_local // block_air
    olev, rows, cols = marine_heat.shape
    m_local, degrees = associated_polynomial_quadrature.shape[1:]
    lon_per, lat_per = lons // grps, lats // grps
    wide = lons * LANES
    vmem = pl.BlockSpec(memory_space=pltpu.VMEM)
    smem = pl.BlockSpec(memory_space=pltpu.SMEM)
    f32, bf16 = jnp.float32, jnp.bfloat16
    dma, dmas = pltpu.SemaphoreType.DMA, lambda n: pltpu.SemaphoreType.DMA((n,))

    lon_ids = y * lon_local + jnp.arange(lon_local, dtype=jnp.int32)
    live = (lon_ids[None, :] < parallel_nodes[:, None]).astype(f32)
    aloft_state = aloft_gridpoint.astype(f32)
    partial_flux = jnp.sum(layer_pressure_share[:, None, None] * aloft_state, axis=0) * live
    partial_flux = jnp.pad(partial_flux, ((0, 0), (0, 3 * LANES - lon_local)))
    inverse = 1.0 / parallel_nodes.astype(f32)

    def by_slot(field):
        split = field.reshape(field.shape[:-1] + (blocks, block_air))
        split = jnp.moveaxis(split, -1, -3)
        pad = [(0, 0)] * (split.ndim - 3) + [(0, 8 - block_air), (0, 0), (0, BLK_PAD - blocks)]
        padded = jnp.pad(split, pad)
        return padded.reshape(-1, lat_count * BLK_PAD)

    sizes = (grps, lats, lons, lat_count, lon_local, m_local, block_air)
    sea_table, flux_table, e1, e2 = pl.pallas_call(
        functools.partial(spread_kernel, sizes),
        out_shape=(
            jax.ShapeDtypeStruct((lats, lon_per, rows, cols), bf16),
            jax.ShapeDtypeStruct((lons, lat_per, 32, LANES), bf16),
            jax.ShapeDtypeStruct((lat_count * BLK_PAD, 2 * wide), bf16),
            jax.ShapeDtypeStruct((lat_count * 8, 2 * wide), f32),
        ),
        in_specs=[smem, smem, vmem, vmem],
        out_specs=(vmem,) * 4,
        scratch_shapes=[
            pltpu.VMEM((rows, cols), bf16),
            pltpu.VMEM((3 * lat_count, LANES), f32),
            pltpu.VMEM((grps, 3 * lat_count, LANES), f32),
            dma,
            dma,
            dma,
            dmas(grps),
            dmas(lons),
            dmas(lon_per),
            dmas(lats),
            dmas(lat_per),
            dmas(lats),
            dmas(lats),
            dmas(lons),
            dmas(lons),
        ],
        compiler_params=pltpu.CompilerParams(
            collective_id=0, has_side_effects=True, vmem_limit_bytes=VMEM_LIMIT
        ),
    )(parallel_nodes, inverse, partial_flux, marine_heat)

    chosen = skin_warmth_feeding_panels.reshape(-1)
    column, row = chosen % lons, chosen // lons
    local = (row // rows) * (lon_per * rows) + (column % lon_per) * rows + row % rows
    local = jnp.where(column // lon_per == g, local, -1)
    table = sea_table.reshape(-1, cols)
    one_hot = (local[:, None] == jnp.arange(table.shape[0], dtype=jnp.int32)[None, :]).astype(bf16)
    picked = jnp.dot(one_hot, table, preferred_element_type=f32).reshape(
        skin_warmth_feeding_panels.shape + (cols,)
    )
    warmth = jnp.sum(skin_warmth_mapping_factors.astype(f32) * picked[:, :, :, None, :], axis=(2, 4))
    warmth = by_slot(warmth.reshape(lat_count, lon_local))

    chosen = heat_feeding_panels.reshape(-1)
    parallel, slot = chosen // (blocks * lons), chosen % (blocks * lons)
    band, lon, block = parallel // lat_count, slot // blocks, slot % blocks
    local = (
        (lon * lat_per + band % lat_per) * 32 + (block // PACK) * lat_count + parallel % lat_count
    )
    local = jnp.where(band // lat_per == g, local, -1)
    table = flux_table.reshape(-1, LANES)
    one_hot = (local[:, None] == jnp.arange(table.shape[0], dtype=jnp.int32)[None, :]).astype(bf16)
    line = jnp.dot(one_hot, table, preferred_element_type=f32)
    lane = jnp.arange(LANES, dtype=jnp.int32)
    line = jnp.where(lane[None, :] // block_air == (block % PACK)[:, None], line, 0.0)
    fold = (lane[:, None] % block_air == jnp.arange(block_air)[None, :]).astype(bf16)
    air = jnp.dot(line.astype(bf16), fold, preferred_element_type=f32)
    air = air.reshape(heat_feeding_panels.shape + (block_air,))
    flux = jnp.sum(
        heat_transfer_factors.astype(f32) * air[..., None], axis=(2, 3)
    ).reshape(rows, cols)

    sizes = (grps, lats, lons, lat_count, levels, m_local, degrees, olev, rows, cols)
    n_local = degrees // lats
    parts = 2 * levels
    width = -(-parts * m_local // LANES) * LANES
    spec, ocean = pl.pallas_call(
        functools.partial(spectral_kernel, sizes),
        out_shape=(
            jax.ShapeDtypeStruct((n_local, width), f32),
            jax.ShapeDtypeStruct((olev, rows, cols), f32),
        ),
        in_specs=[smem, smem] + [vmem] * 9,
        out_specs=(vmem, vmem),
        scratch_shapes=[
            pltpu.VMEM((grps, 8, lat_count * BLK_PAD), f32),
            pltpu.VMEM((grps, rows, cols), f32),
            pltpu.VMEM((olev + 1, rows + 16, cols + 2 * LANES), f32),
            pltpu.VMEM((lons, parts * lat_count, LANES), f32),
            pltpu.VMEM((lons, parts * lat_count, LANES), f32),
            pltpu.VMEM((parts * lat_count, m_local, LANES), f32),
            pltpu.VMEM((width, LANES), f32),
            pltpu.VMEM((degrees, width), bf16),
            pltpu.VMEM((lats, n_local, width), bf16),
            dmas(grps),
            dmas(grps),
            dma,
            dmas(grps),
            dmas(8),
            dmas(8),
            dmas(lons),
            dmas(lons),
            dmas(lats),
            dmas(lats),
        ],
        compiler_params=pltpu.CompilerParams(
            collective_id=1, has_side_effects=True, vmem_limit_bytes=VMEM_LIMIT
        ),
    )(
        layer_sensitivity,
        inverse,
        warmth,
        flux,
        by_slot(aloft_state * live),
        by_slot(live[None]),
        e1,
        e2,
        associated_polynomial_quadrature,
        marine_heat,
        water_indicator,
    )
    spectra = spec[:, : parts * m_local].reshape(n_local, parts, m_local)
    return (spectra, ocean)


def solution(mesh):
    in_specs = (
        P("grp", "lat", "lon"),
        P("lat"),
        P("grp"),
        P("grp"),
        P("lat", "lon", None),
        P("grp", "lat", "lon"),
        P("lat", "lon"),
        P("lat", "lon", None),
        P("lat", "lon", None, None, None),
        P("lat", "lon", None),
        P("lat", "lon", None, None, None),
    )
    out_specs = (P("lat", "grp", "lon"), P("grp", "lat", "lon"))
    return jax.shard_map(
        per_device, mesh=mesh, in_specs=in_specs, out_specs=out_specs, check_vma=False
    )
```

time: 499 us -> 97.5 us (0.20)
  waiting for transfers between devices: 122 us -> 0 us
  blocking collectives: 114 us -> 0 us
  local copies, waits for them, and re-layouts: 109 us -> 6.11 us
  other arithmetic: 105 us -> 11.6 us
  Pallas kernels: 0 us -> 77.4 us
  loops' own time: 14.7 us -> 0 us
  between operations: 14.1 us -> 0.82 us
  starting transfers between devices: 11.1 us -> 0 us
  matrix products: 6.58 us -> 1.16 us
    all_gather x3 -> x0, blocking collectives: 99.6 us -> none  [the longest x1 46.6 us: per_device(): lax.all_gather(band_flux.astype(jnp.bfloat16), 'lat', axis=0, tiled=True)]
    convert_element_type x8 -> x1, other arithmetic: 91.8 us -> 0.73 us  [per_device(): live = (lon_ids[None, :] < parallel_nodes[:, None]).astype(f32)]
    pallas_call x0 -> x2, Pallas kernels: none -> 77.4 us  [the longest x1 46.5 us: per_device(): pl.pallas_call(functools.partial(spectral_kernel, sizes), out_shape=(jax....]
    all_gather x1 -> x0, waiting for transfers between devices: 76 us -> none  [per_device(): entire_ocean_field = lax.all_gather(band_sea, 'lat', axis=0, tiled=True)]
    unnamed x26 -> x18, local copies, waits for them, and re-layouts: 69.1 us -> 3.8 us
    unnamed x5 -> x0, waiting for transfers between devices: 37.6 us -> none
    reshape x13 -> x5, local copies, waits for them, and re-layouts: 20.4 us -> 1.25 us  [the longest x1 0.81 us: per_device(): spectra = spec[:, :parts * m_local].reshape(n_local, parts, m_local)]
    another operation x1 -> x0, loops' own time: 14.7 us -> none  [per_device(): per_lat = lax.map(one_lat, (forced_lat, parallel_nodes))]
  transfers between devices with their start and end apart: 7 -> 0, of which waited for: 5 -> 0; matrix products, arithmetic and copies ran while one was open for 6% -> 0% of each run, Pallas kernels for 0% -> 0%
where the time goes in v1:
time: 97.5 us; the launch traced here: 97.1 us
  Pallas kernels  77.4 us (79%)
  other arithmetic  11.6 us (12%)
  local copies, waits for them, and re-layouts  6.11 us (6%)
  matrix products  1.16 us (1%)
    pallas_call x1, Pallas kernels, per_device(): pl.pallas_call(functools.partial(spectral_kernel, sizes), out_shape=(jax....  46.5 us
    pallas_call x1, Pallas kernels, per_device(): pl.pallas_call(functools.partial(spread_kernel, sizes), out_shape=(jax.Sh...  30.9 us
    reduce_sum x1, other arithmetic, per_device(): jnp.sum(skin_warmth_mapping_factors.astype(f32) * picked[:, :, :, None, :...  5.08 us
    unnamed x18, local copies, waits for them, and re-layouts  3.8 us

profile of v1, /device:TPU:6, one launch (start us, length us, event | category | flops | bytes accessed | tf_op | source)
XLA Modules:
  0.0 97.1 jit_solution(18039814063601373109)
XLA Ops:
  0.6 0.7 compare_convert_fusion
  1.4 0.8 convert_multiply_fusion
  2.2 0.7 compare_select_fusion.1
  2.9 0.7 convert_divide_fusion.inverse_ref
  3.6 0.0 copy-start.1
  3.6 0.8 copy-done.1
  4.4 0.0 copy-start.4
  4.4 0.7 copy-done.4
  5.1 30.9 %shard_map.122 = (bf16[16,2,32,128]{3,2,1,0:T(8,128)(2,1)S(1)}, bf16[8,4,32,128]{3,2,1,0:T(8,128)(2,1)S(1)}, bf16[512,2048]{1,0:T(8,128)(2,1)S(1)}, f32[64,2048]{1,0:T(8,128)S(1)}) custom-call(s32[8]{0:T(128)S(1)} %copy-done.4, f32[8]{0:T(128)S(1)} %convert_divide_fusion.inverse_ref, f32[8,384]{1,0:T(8,128)S(1)} %pad.17.partial_ref, f32[4,32,128]{2,1,0:T(8,128)S(1)} %copy-done.1), custom_call_target="tpu_custom_call" | custom-call | tf_op jit(solution)/shard_map/pallas_call | solution.py:526
  36.0 0.7 broadcast_divide_fusion
  36.6 0.1 copy.27
  36.7 0.1 rem.212
  36.9 0.1 copy.29
  37.0 0.1 div.107
  37.1 0.7 sign_compare_fusion
  37.8 0.1 copy.28
  37.9 0.1 ne.302
  38.0 0.4 fusion.5
  38.4 0.1 mul.97
  38.6 0.0 copy-start.7
  38.6 0.1 copy.30
  38.7 1.3 %multiply_reduce_fusion.1.flux_ref = f32[32,128]{1,0:T(8,128)S(1)} fusion(bf16[32,1,4,6,128]{4,2,3,1,0:T(4,128)(2,1)} %param.19, f32[32,4,6]{1,2,0:T(8,128)S(1)} %copy.30), kind=kLoop, calls=%fused_computation.9 | loop fusion | flops 290816 | bytes 216064 | tf_op jit(solution)/shard_map/reduce_sum | solution.py:585
  40.0 0.8 compare_select_fusion
  40.8 0.8 fusion.1
  41.5 0.2 copy.25
  41.8 0.0 copy-done.7
  41.8 0.0 copy-start.5
  41.8 0.0 copy-start.2
  41.8 0.0 copy-start.3
  41.8 0.0 copy-start.6
  41.8 5.1 %multiply_reduce_fusion = f32[8,54,6]{2,1,0:T(8,128)S(1)} fusion(bf16[8,54,2,6,128]{4,2,3,1,0:T(2,128)(2,1)S(1)} %copy-done.7, f32[8,54,2,128]{3,2,1,0:T(2,128)S(1)} %copy.25), kind=kLoop, calls=%fused_computation.3 | loop fusion | flops 1988064 | bytes 1779840 | tf_op jit(solution)/shard_map/reduce_sum | solution.py:567
  46.9 0.1 copy.33.warmth_ref
  47.0 0.2 reshape.367
  47.2 0.2 copy.34
  47.5 0.1 reshape.368.aloft_ref
  47.6 0.0 copy-done.5
  47.6 0.1 compare_bitcast_fusion
  47.6 0.1 reshape.373.mask_ref
  47.7 0.0 copy-done.2
  47.7 0.0 copy-done.3
  47.7 0.0 copy-done.6
  47.7 0.0 copy-start
  47.7 1.4 %copy-done = bf16[8,80,1280]{2,1,0:T(8,128)(2,1)S(1)} copy-done((bf16[8,80,1280]{2,1,0:T(8,128)(2,1)S(1)}, bf16[8,80,1280]{2,1,0:T(8,128)(2,1)}, u32[]{:S(2)}) %copy-start) | copy-done | bytes 1638424
  49.2 46.5 %shard_map.123 = (f32[80,384]{1,0:T(8,128)S(1)}, f32[4,32,128]{2,1,0:T(8,128)S(1)}) custom-call(f32[2]{0:T(128)S(1)} %copy-done.6, f32[8]{0:T(128)S(1)} %convert_divide_fusion.inverse_ref, f32[8,512]{1,0:T(8,128)S(1)} %copy.33.warmth_ref, f32[32,128]{1,0:T(8,128)S(1)} %multiply_reduce_fusion.1.flux_ref, f32[16,512]{1,0:T(8,128)S(1)} %reshape.368.aloft_ref, ...), custom_call_target="tpu_custom_call" | custom-call | tf_op jit(solution)/shard_map/pallas_call | solution.py:593
  95.7 0.8 reshape.371
  96.5 0.6 copy.36
  (9 shorter events, 0.1 us)
Async XLA Ops:
  3.6 0.8 copy-start.1
  4.4 0.7 copy-start.4
  38.6 3.2 %copy-start.7 = (bf16[8,54,2,6,128]{4,2,3,1,0:T(2,128)(2,1)S(1)}, bf16[8,54,2,6,128]{4,2,3,1,0:T(2,128)(2,1)}, u32[]{:S(2)}) copy-start(bf16[8,54,2,6,128]{4,2,3,1,0:T(2,128)(2,1)} %param.21) | copy-start | bytes 3981316
  41.8 5.8 %copy-start.5 = (s32[8]{0:T(128)S(1)}, s32[8]{0:T(128)}, u32[]{:S(2)}) copy-start(s32[8]{0:T(128)} %nodes_ref.1) | copy-start | bytes 100
  41.8 5.9 %copy-start.2 = (f32[4,32,128]{2,1,0:T(8,128)S(1)}, f32[4,32,128]{2,1,0:T(8,128)}, u32[]{:S(2)}) copy-start(f32[4,32,128]{2,1,0:T(8,128)} %heat_ref.3) | copy-start | bytes 196612
  41.8 5.9 %copy-start.3 = (s32[32,128]{1,0:T(8,128)S(1)}, s32[32,128]{1,0:T(8,128)}, u32[]{:S(2)}) copy-start(s32[32,128]{1,0:T(8,128)} %water_ref.1) | copy-start | bytes 49156
  41.8 5.9 %copy-start.6 = (f32[2]{0:T(128)S(1)}, f32[2]{0:T(128)}, u32[]{:S(2)}) copy-start(f32[2]{0:T(128)} %sens_ref.1) | copy-start | bytes 28
  47.7 1.4 %copy-start = (bf16[8,80,1280]{2,1,0:T(8,128)(2,1)S(1)}, bf16[8,80,1280]{2,1,0:T(8,128)(2,1)}, u32[]{:S(2)}) copy-start(bf16[8,80,1280]{2,1,0:T(8,128)(2,1)} %quad_ref.1) | copy-start | bytes 4915204

commit v2 on v0

v2 whole, which is shorter than its diff:
```python
import functools
import math

import jax
import jax.numpy as jnp
from jax import lax
from jax.experimental import pallas as pl
from jax.experimental.pallas import tpu as pltpu
from jax.sharding import PartitionSpec as P

TWO_PI = 6.283185307179586
FLUX_RATE = 0.5
KAPPA = 0.2
MESH_ID = pl.DeviceIdType.MESH
LANES = 128
BLK_PAD = 64
VMEM_LIMIT = 48 * 1024 * 1024


def shifted(index, offset, count):
    return lax.rem(index + offset, count)


def greet(partners):
    barrier = pltpu.get_barrier_semaphore()
    for partner in partners:
        pl.semaphore_signal(barrier, inc=1, device_id=partner, device_id_type=MESH_ID)
    pl.semaphore_wait(barrier, len(partners))


def remote(src, dst, send_sem, recv_sem, partner):
    return pltpu.make_async_remote_copy(
        src_ref=src,
        dst_ref=dst,
        send_sem=send_sem,
        recv_sem=recv_sem,
        device_id=partner,
        device_id_type=MESH_ID,
    )


def landed(ref, sem):
    pltpu.make_async_copy(ref, ref, sem).wait()


def turn(phase, count, inverse):
    rest = phase - jnp.floor(phase * inverse + 0.5) * count
    part = rest * inverse
    square = part * part
    cosine = jnp.zeros_like(part)
    sine = jnp.zeros_like(part)
    for power in range(8, -1, -1):
        sign = -1.0 if power % 2 else 1.0
        cosine = cosine * square + sign * TWO_PI ** (2 * power) / math.factorial(2 * power)
        sine = sine * square - sign * TWO_PI ** (2 * power + 1) / math.factorial(2 * power + 1)
    return cosine, sine * part


def step_kernel(
    sizes,
    nodes_hbm,
    share_hbm,
    sens_hbm,
    quad_hbm,
    warm_hbm,
    cool_hbm,
    aloft_ref,
    heat_ref,
    water_ref,
    warm_ids_ref,
    cool_ids_ref,
    spec_ref,
    ocean_ref,
    nodes_ref,
    share_ref,
    sens_ref,
    quad_ref,
    warm_ref,
    cool_ref,
    sea_ref,
    flux_ref,
    e1_ref,
    e2_ref,
    stage,
    part,
    gathered,
    warmth_out,
    warmth_in,
    flux_out,
    flux_in,
    ext,
    waves,
    waves_in,
    fourier,
    quad_out,
    quad_in,
    sums,
    local_sems,
    own_sem,
    sea1_send,
    sea1_recv,
    flux0_send,
    flux0_recv,
    flux1_send,
    flux1_recv,
    sea2_send,
    sea2_recv,
    flux2_send,
    flux2_recv,
    warmth_send,
    warmth_recv,
    fluxp_send,
    fluxp_recv,
    halo_send,
    halo_recv,
    waves_send,
    waves_recv,
    fourier_send,
    fourier_recv,
    quad_send,
    quad_recv,
    pass_send,
    pass_recv,
):
    (grps, lats, lons, lat_count, levels, lon_local, block_air, m_local, degrees, olev, rows, cols) = sizes
    g, t, y = (lax.axis_index(name) for name in ("grp", "lat", "lon"))
    f32, bf16, i32 = jnp.float32, jnp.bfloat16, jnp.int32
    wide = lons * LANES
    blocks = lon_local // block_air
    parts = 2 * levels
    n_local = degrees // lats
    line = lat_count * BLK_PAD
    lon_per, lat_per = lons // grps, lats // grps
    sea_owner, yy = y // lon_per, lax.rem(y, lon_per)
    flux_owner, tt = t // lat_per, lax.rem(t, lat_per)
    core = lax.rem(g, 2)
    sibling = {"grp": g + 1 - 2 * core}
    north, south = shifted(t, lats - 1, lats), shifted(t, 1, lats)
    west, east = shifted(y, lons - 1, lons), shifted(y, 1, lons)
    mid_rows, mid_cols = slice(8, 8 + rows), slice(LANES, LANES + cols)
    first_rows, last_rows = slice(8, 16), slice(rows, rows + 8)
    low_rows, high_rows = slice(0, 8), slice(8 + rows, 16 + rows)
    low_cols, high_cols = slice(0, LANES), slice(LANES + cols, 2 * LANES + cols)
    halo = [
        ({"lat": south}, last_rows, low_rows, mid_cols),
        ({"lat": north}, first_rows, high_rows, mid_cols),
        ({"lon": east}, mid_rows, mid_rows, low_cols),
        ({"lon": west}, mid_rows, mid_rows, high_cols),
        ({"lat": south, "lon": east}, last_rows, low_rows, low_cols),
        ({"lat": south, "lon": west}, last_rows, low_rows, high_cols),
        ({"lat": north, "lon": east}, first_rows, high_rows, low_cols),
        ({"lat": north, "lon": west}, first_rows, high_rows, high_cols),
    ]
    pairs = lats // 2
    early = 5 * pairs // 8

    fetches = [
        pltpu.make_async_copy(src, dst, local_sems.at[k])
        for k, (src, dst) in enumerate(
            (
                (nodes_hbm, nodes_ref),
                (share_hbm, share_ref),
                (sens_hbm, sens_ref),
                (quad_hbm, quad_ref),
                (cool_hbm, cool_ref),
                (warm_hbm, warm_ref),
            )
        )
    ]
    for fetch in fetches:
        fetch.start()

    stage[...] = heat_ref[0].astype(bf16)
    for level in range(olev):
        ext[level, mid_rows, mid_cols] = heat_ref[level]
    wet_mid = water_ref[...].astype(f32)
    ext[olev, mid_rows, mid_cols] = wet_mid

    for fetch in fetches[:3]:
        fetch.wait()
    lane = lax.broadcasted_iota(i32, (8, line), 1)
    slot = lax.broadcasted_iota(i32, (8, line), 0)
    block = lane % BLK_PAD
    limit = jnp.zeros((8, line), i32)
    for i in range(lat_count):
        limit = jnp.where(lane // BLK_PAD == i, nodes_ref[i], limit)
    live = (block < blocks) & (slot < block_air)
    live = live & (y * lon_local + block * block_air + slot < limit)
    flux_sum = share_ref[0] * aloft_ref[0:8, :]
    for l in range(1, levels):
        flux_sum = flux_sum + share_ref[l] * aloft_ref[8 * l : 8 * l + 8, :]
    flux_sum = jnp.where(live, flux_sum, 0.0)
    tiles = line // LANES
    for k in range(tiles):
        part[8 * k : 8 * k + 8, :] = flux_sum[:, k * LANES : (k + 1) * LANES]

    greet(
        [{"grp": shifted(g, d, grps)} for d in range(1, grps)]
        + [{"lon": shifted(y, d, lons)} for d in range(1, lons)]
        + [{"lat": shifted(t, d, lats)} for d in range(1, lats)]
        + [
            {"grp": shifted(g, d, grps), "lon": shifted(y, e, lons)}
            for d in range(1, grps)
            for e in range(1, lons)
        ]
        + [partner for partner, _, _, _ in halo[4:]]
    )

    @pl.when(g == 0)
    def _():
        for d in range(1, lons):
            remote(
                stage,
                sea_ref.at[t, yy],
                sea1_send.at[d],
                sea1_recv.at[yy],
                {"grp": sea_owner, "lon": shifted(y, d, lons)},
            ).start()

    @pl.when((g == 0) & (sea_owner != 0))
    def _():
        remote(
            stage, sea_ref.at[t, yy], sea1_send.at[0], sea1_recv.at[yy], {"grp": sea_owner}
        ).start()

    @pl.when((g == 0) & (sea_owner == 0))
    def _():
        sea_ref[t, yy] = stage[...]

    @pl.when(g != flux_owner)
    def _():
        remote(
            part, gathered.at[g], flux0_send, flux0_recv.at[g], {"grp": flux_owner}
        ).start()

    def offset_of(rank):
        half = jnp.where(rank % 2 == 1, (rank + 1) // 2, pairs - rank // 2)
        return 2 * lax.rem(half, pairs) + core

    def pack(rank):
        other = shifted(t, offset_of(rank), lats)
        start = other * n_local
        first = jnp.minimum(start // LANES, degrees // LANES - 2)
        offset = start - first * LANES
        lanes = pl.ds(pl.multiple_of(first * LANES, LANES), 2 * LANES)
        at = lax.broadcasted_iota(i32, (16, 2 * LANES), 1)

        def some_rows(b, carry):
            own = pl.ds(pl.multiple_of(b * 16, 16), 16)
            out = [jnp.zeros((16, LANES), f32) for _ in range(lat_count * n_local // LANES + 1)]
            for i in range(lat_count):
                tile, inner = divmod(i * n_local, LANES)
                window = quad_ref[i, own, lanes].astype(f32)
                window = pltpu.roll(window, lax.rem(inner - offset + 2 * LANES, 2 * LANES), 1)
                window = jnp.where((at >= inner) & (at < inner + n_local), window, 0.0)
                out[tile] = out[tile] + window[:, :LANES]
                if inner + n_local > LANES:
                    out[tile + 1] = out[tile + 1] + window[:, LANES:]
            for k in range(lat_count * n_local // LANES):
                quad_out[rank, own, k * LANES : (k + 1) * LANES] = out[k].astype(bf16)
            return carry

        lax.fori_loop(0, m_local // 16, some_rows, 0)

    def quad_copy(rank):
        return remote(
            quad_out.at[rank],
            quad_in.at[t],
            quad_send.at[rank],
            quad_recv.at[t],
            {"lat": shifted(t, offset_of(rank), lats)},
        )

    own_copy = pltpu.make_async_copy(quad_out.at[0], quad_in.at[t], own_sem)

    def pack_and_send(rank, carry):
        pack(rank)

        @pl.when((rank == 0) & (core == 0))
        def _():
            own_copy.start()

        @pl.when((rank != 0) | (core != 0))
        def _():
            quad_copy(rank).start()

        return carry

    fetches[3].wait()
    lax.fori_loop(0, early, pack_and_send, 0)

    for k in range(lon_per):
        @pl.when((g != 0) | (lon_per * g + k != y))
        def _():
            landed(sea_ref.at[t, k], sea1_recv.at[k])

    for d in range(1, lats):
        remote(
            sea_ref.at[t],
            sea_ref.at[t],
            sea2_send.at[d],
            sea2_recv.at[t],
            {"lat": shifted(t, d, lats)},
        ).start()

    @pl.when(g == flux_owner)
    def _():
        gathered[g] = part[...]
        for d in range(1, grps):
            other = shifted(g, d, grps)
            landed(gathered.at[other], flux0_recv.at[other])
        total = gathered[0]
        for other in range(1, grps):
            total = total + gathered[other]
        flux_ref[y, tt] = total.astype(bf16)
        for d in range(1, lats):
            remote(
                flux_ref.at[y, tt],
                flux_ref.at[y, tt],
                flux1_send.at[d],
                flux1_recv.at[tt],
                {"lat": shifted(t, d, lats)},
            ).start()

    def tables(i, carry):
        count = jnp.full((8, LANES), nodes_ref[i], i32).astype(f32)
        inverse = jnp.concatenate([1.0 / count] * lons, axis=1)
        count = jnp.concatenate([count] * lons, axis=1)
        lane = lax.broadcasted_iota(i32, (8, wide), 1)
        row_f = lax.broadcasted_iota(i32, (8, wide), 0).astype(f32)
        inner = lane % LANES
        wave_f = ((lane // LANES) * m_local + inner).astype(f32)
        base_f = (y * lon_local).astype(f32)
        high = turn((base_f + 8 * block_air * row_f) * wave_f, count, inverse)
        low = turn((block_air * row_f) * wave_f, count, inverse)
        fine = turn(row_f * wave_f, count, inverse)
        usable = (inner < m_local) & (2.0 * wave_f < count)
        own = pl.ds(pl.multiple_of(i * 8, 8), 8)
        e2_ref[own, :wide] = jnp.where(usable, fine[0] * inverse, 0.0)
        e2_ref[own, wide:] = jnp.where(usable, fine[1] * inverse, 0.0)
        for pair in range(BLK_PAD // 16):
            real, imag = [], []
            for b in (2 * pair, 2 * pair + 1):
                hr, hi = high[0][b : b + 1], high[1][b : b + 1]
                real.append(hr * low[0] - hi * low[1])
                imag.append(hr * low[1] + hi * low[0])
            where = pl.ds(pl.multiple_of(i * BLK_PAD + pair * 16, 16), 16)
            e1_ref[where, :wide] = jnp.concatenate(real, axis=0).astype(bf16)
            e1_ref[where, wide:] = jnp.concatenate(imag, axis=0).astype(bf16)
        return carry

    lax.fori_loop(0, lat_count // 2, tables, 0)

    for k in range(lat_per):
        @pl.when(g * lat_per + k != t)
        def _():
            landed(flux_ref.at[y, k], flux1_recv.at[k])

    for d in range(1, lons):
        remote(
            flux_ref.at[y],
            flux_ref.at[y],
            flux2_send.at[d],
            flux2_recv.at[y],
            {"lon": shifted(y, d, lons)},
        ).start()

    lax.fori_loop(lat_count // 2, lat_count, tables, 0)

    for d in range(1, lats):
        other = shifted(t, d, lats)
        landed(sea_ref.at[other], sea2_recv.at[other])

    count_rows = lats * lon_per * rows
    table = sea_ref[...].reshape(count_rows, cols).astype(f32)
    table = jnp.concatenate(
        [jnp.transpose(table[k : k + LANES]) for k in range(0, count_rows, LANES)], axis=1
    ).astype(bf16)
    picks = 2 * blocks
    chosen = warm_ids_ref[...]
    column, row = chosen % lons, chosen // lons
    spot = (row // rows) * (lon_per * rows) + (column % lon_per) * rows + row % rows
    spot = jnp.where((column // lon_per == g) & (chosen >= 0), spot, -1)
    fetches[5].wait()
    table_row = lax.broadcasted_iota(i32, (count_rows, LANES), 0)
    pick_id = lax.broadcasted_iota(i32, (picks, 8, LANES), 0)
    pick_lane = lax.broadcasted_iota(i32, (picks, 8, LANES), 2)
    diagonal = pick_lane == (pick_id % 2) * BLK_PAD + pick_id // 2
    out_lane = lax.broadcasted_iota(i32, (8, LANES), 1)
    fill = jnp.zeros((picks, 8 - block_air, LANES), f32)
    warm_sums = []
    for i in range(lat_count):
        one_hot = jnp.where(table_row == spot[i : i + 1, :], 1.0, 0.0).astype(bf16)
        picked = jnp.dot(table, one_hot, preferred_element_type=f32).astype(bf16)
        factor = warm_ref[picks * i : picks * (i + 1)].astype(f32)
        factor = jnp.concatenate([factor, fill], axis=1).reshape(picks * 8, LANES).astype(bf16)
        product = jnp.dot(factor, picked, preferred_element_type=f32)
        product = product.reshape(picks, 8, LANES)
        total = jnp.sum(jnp.where(diagonal, product, 0.0), axis=0)
        warm_sums.append(total + pltpu.roll(total, BLK_PAD, 1))
    for k in range(tiles):
        warmth_out[:, k * LANES : (k + 1) * LANES] = jnp.where(
            out_lane < BLK_PAD, warm_sums[2 * k], warm_sums[2 * k + 1]
        )
    for d in range(1, grps):
        remote(
            warmth_out,
            warmth_in.at[g],
            warmth_send.at[d],
            warmth_recv.at[g],
            {"grp": shifted(g, d, grps)},
        ).start()

    lax.fori_loop(early, pairs, pack_and_send, 0)

    for d in range(1, lons):
        other = shifted(y, d, lons)
        landed(flux_ref.at[other], flux2_recv.at[other])
    chosen = cool_ids_ref[0:1, :]
    parallel, place = chosen // (blocks * lons), chosen % (blocks * lons)
    band, within = parallel // lat_count, parallel % lat_count
    lon, blk = place // blocks, place % blocks
    group = (lon * lat_per + band % lat_per) * tiles + within // 2
    group = jnp.where(band // lat_per == g, group, -1)
    spot = (within % 2) * BLK_PAD + blk
    group_count = lons * lat_per * tiles
    one_hot = jnp.where(
        lax.broadcasted_iota(i32, (LANES, LANES), 0) == spot, 1.0, 0.0
    ).astype(bf16)
    found = jnp.dot(
        flux_ref[...].reshape(group_count * 8, LANES), one_hot, preferred_element_type=f32
    ).reshape(group_count, 8, LANES)
    group_id = lax.broadcasted_iota(i32, (group_count, 8, LANES), 0)
    air = jnp.sum(jnp.where(group_id == group[None], found, 0.0), axis=0)
    width = LANES * 8
    repeat = jnp.where(
        lax.broadcasted_iota(i32, (LANES, width), 0)
        == lax.broadcasted_iota(i32, (LANES, width), 1) // 8,
        1.0,
        0.0,
    ).astype(bf16)
    air = jnp.dot(air.astype(bf16), repeat, preferred_element_type=f32)
    own_slot = lax.broadcasted_iota(i32, (8, width), 1) % 8 == lax.broadcasted_iota(
        i32, (8, width), 0
    )
    air = jnp.sum(jnp.where(own_slot, air, 0.0), axis=0, keepdims=True)
    per_row = width // rows
    air = jnp.where(
        lax.broadcasted_iota(i32, (rows, width), 1) // per_row
        == lax.broadcasted_iota(i32, (rows, width), 0),
        air,
        0.0,
    ).astype(bf16)
    fetches[4].wait()
    factor = cool_ref[...].astype(f32)
    factor = jnp.concatenate(
        [factor, jnp.zeros((LANES, 8 - block_air, LANES), f32)], axis=1
    ).reshape(width, LANES)
    flux_out[...] = jnp.dot(air, factor.astype(bf16), preferred_element_type=f32)

    @pl.when(g != 0)
    def _():
        remote(
            flux_out, flux_in.at[g], fluxp_send, fluxp_recv.at[g], {"grp": jnp.int32(0)}
        ).start()

    warmth_in[g] = warmth_out[...]
    for d in range(1, grps):
        other = shifted(g, d, grps)
        landed(warmth_in.at[other], warmth_recv.at[other])
    warmth = warmth_in[0]
    for other in range(1, grps):
        warmth = warmth + warmth_in[other]
    forced = jnp.concatenate(
        [
            jnp.where(live, aloft_ref[8 * l : 8 * l + 8, :] + sens_ref[l] * warmth, 0.0)
            for l in range(levels)
        ],
        axis=0,
    )
    lane = lax.broadcasted_iota(i32, forced.shape, 1)
    stacked = jnp.concatenate(
        [jnp.where(lane // BLK_PAD == i, forced, 0.0) for i in range(lat_count)], axis=0
    ).astype(bf16)
    real = jnp.dot(stacked, e1_ref[:, :wide], preferred_element_type=f32)
    imag = jnp.dot(stacked, e1_ref[:, wide:], preferred_element_type=f32)
    for i in range(lat_count):
        slot_r = e2_ref[8 * i : 8 * i + 8, :wide]
        slot_i = e2_ref[8 * i : 8 * i + 8, wide:]
        for l in range(levels):
            at = (i * levels + l) * 8
            re, im = real[at : at + 8], imag[at : at + 8]
            out_r = jnp.sum(re * slot_r - im * slot_i, axis=0, keepdims=True)
            out_i = jnp.sum(re * slot_i + im * slot_r, axis=0, keepdims=True)
            for c, out in enumerate((out_r, out_i)):
                row = (2 * l + c) * lat_count + i
                for k in range(lons):
                    waves[k, row : row + 1, :] = out[:, k * LANES : (k + 1) * LANES]

    for d in range(1, lons):
        other = shifted(y, d, lons)
        remote(
            waves.at[other], waves_in.at[y], waves_send.at[d], waves_recv.at[y], {"lon": other}
        ).start()

    @pl.when(g == 0)
    def _():
        total = flux_out[...]
        for other in range(1, grps):
            landed(flux_in.at[other], fluxp_recv.at[other])
            total = total + flux_in[other]
        ext[0, mid_rows, mid_cols] = heat_ref[0] + FLUX_RATE * total * wet_mid

    for index, (partner, src_rows, dst_rows, dst_cols) in enumerate(halo):
        remote(
            ext.at[:, src_rows, mid_cols],
            ext.at[:, dst_rows, dst_cols],
            halo_send.at[index],
            halo_recv.at[index],
            partner,
        ).start()

    waves_in[y] = waves[y]
    for d in range(1, lons):
        other = shifted(y, d, lons)
        landed(waves_in.at[other], waves_recv.at[other])
    total = waves_in[0]
    for other in range(1, lons):
        total = total + waves_in[other]
    fourier[t] = total.astype(bf16)
    for d in range(1, lats):
        remote(
            fourier.at[t],
            fourier.at[t],
            fourier_send.at[d],
            fourier_recv.at[t],
            {"lat": shifted(t, d, lats)},
        ).start()

    def source(rank):
        return shifted(t, lats - offset_of(rank), lats)

    def pass_on(rank, carry):
        @pl.when((rank == 0) & (core == 0))
        def _():
            own_copy.wait()

        @pl.when((rank != 0) | (core != 0))
        def _():
            landed(quad_in.at[source(rank)], quad_recv.at[source(rank)])

        remote(
            quad_in.at[source(rank)],
            quad_in.at[source(rank)],
            pass_send.at[rank],
            pass_recv.at[source(rank)],
            sibling,
        ).start()
        return carry

    lax.fori_loop(0, pairs, pass_on, 0)

    for index, (partner, src_rows, dst_rows, dst_cols) in enumerate(halo):
        landed(ext.at[:, dst_rows, dst_cols], halo_recv.at[index])
    shape = (rows + 16, cols + 2 * LANES)
    row_id = lax.broadcasted_iota(i32, shape, 0) + (t * rows - 8)
    col_id = lax.broadcasted_iota(i32, shape, 1) + (y * cols - LANES)
    inside = (row_id >= 0) & (row_id < rows * lats) & (col_id >= 0) & (col_id < cols * lons)
    wet = jnp.where(inside, ext[olev], 0.0)
    moves = ((1, 0), (shape[0] - 1, 0), (1, 1), (shape[1] - 1, 1))
    wet_near = [pltpu.roll(wet, shift, axis) for shift, axis in moves]
    for level in range(olev):
        field = ext[level]
        for _ in range(2):
            total = jnp.zeros_like(field)
            for (shift, axis), near in zip(moves, wet_near):
                total = total + near * (pltpu.roll(field, shift, axis) - field)
            field = field + KAPPA * wet * total
        ocean_ref[level] = field[mid_rows, mid_cols]

    for d in range(1, lats):
        other = shifted(t, d, lats)
        landed(fourier.at[other], fourier_recv.at[other])
    coefs = [fourier[k].astype(f32) for k in range(lats)]
    columns = []
    for a in range(parts):
        tall = jnp.concatenate(
            [coef[a * lat_count : (a + 1) * lat_count] for coef in coefs], axis=0
        )
        columns.append(jnp.transpose(tall)[:m_local])
    columns = jnp.concatenate(columns, axis=0)
    span = lat_count * n_local
    repeat = jnp.where(
        lax.broadcasted_iota(i32, (lats * lat_count, span), 0) % lat_count
        == lax.broadcasted_iota(i32, (lats * lat_count, span), 1) // n_local,
        1.0,
        0.0,
    ).astype(bf16)
    lane = lax.broadcasted_iota(i32, columns.shape, 1)
    sums[...] = jnp.zeros_like(sums)

    def add_source(s):
        own = jnp.where(lane // lat_count == s, columns, 0.0).astype(bf16)
        coef = jnp.dot(own, repeat, preferred_element_type=f32)
        quad = quad_in[s].astype(f32)
        for a in range(parts):
            at = slice(a * m_local, (a + 1) * m_local)
            sums[at, :] = sums[at, :] + coef[at] * quad

    def add_direct(rank, carry):
        add_source(source(rank))
        return carry

    def add_passed(rank, carry):
        s = shifted(source(rank), lats - 1 + 2 * core, lats)
        landed(quad_in.at[s], pass_recv.at[s])
        add_source(s)
        return carry

    lax.fori_loop(0, pairs, add_direct, 0)
    lax.fori_loop(0, pairs, add_passed, 0)

    folded = jnp.zeros((parts * m_local, LANES), f32)
    for i in range(lat_count):
        tile, inner = divmod(i * n_local, LANES)
        if inner + n_local > LANES:
            window = sums[:, tile * LANES : (tile + 2) * LANES]
            folded = folded + pltpu.roll(window, 2 * LANES - inner, 1)[:, :LANES]
        else:
            window = sums[:, tile * LANES : (tile + 1) * LANES]
            folded = folded + (pltpu.roll(window, LANES - inner, 1) if inner else window)
    width = spec_ref.shape[1]
    folded = jnp.concatenate(
        [folded, jnp.zeros((width - parts * m_local, LANES), f32)], axis=0
    )
    result = jnp.transpose(folded)[:n_local]
    lane = lax.broadcasted_iota(i32, result.shape, 1)
    degree = lax.broadcasted_iota(i32, result.shape, 0) + t * n_local
    spec_ref[...] = jnp.where(degree >= lane % m_local + y * m_local, result, 0.0)

    @pl.when(g == 0)
    def _():
        for d in range(1, lons):
            landed(stage, sea1_send.at[d])

    @pl.when((g == 0) & (sea_owner != 0))
    def _():
        landed(stage, sea1_send.at[0])

    @pl.when(g != flux_owner)
    def _():
        landed(part, flux0_send)

    @pl.when(g == flux_owner)
    def _():
        for d in range(1, lats):
            landed(flux_ref.at[y, tt], flux1_send.at[d])

    @pl.when(g != 0)
    def _():
        landed(flux_out, fluxp_send)

    for d in range(1, lats):
        landed(sea_ref.at[t], sea2_send.at[d])
        landed(fourier.at[t], fourier_send.at[d])
    for d in range(1, lons):
        landed(flux_ref.at[y], flux2_send.at[d])
        landed(waves.at[0], waves_send.at[d])
    for d in range(1, grps):
        landed(warmth_out, warmth_send.at[d])
    for index, (partner, src_rows, dst_rows, dst_cols) in enumerate(halo):
        landed(ext.at[:, src_rows, mid_cols], halo_send.at[index])

    def sent(rank, carry):
        @pl.when((rank != 0) | (core != 0))
        def _():
            landed(quad_out.at[rank], quad_send.at[rank])

        landed(quad_in.at[0], pass_send.at[rank])
        return carry

    lax.fori_loop(0, pairs, sent, 0)


def per_device(
    aloft_gridpoint,
    parallel_nodes,
    layer_pressure_share,
    layer_sensitivity,
    associated_polynomial_quadrature,
    marine_heat,
    water_indicator,
    heat_feeding_panels,
    heat_transfer_factors,
    skin_warmth_feeding_panels,
    skin_warmth_mapping_factors,
):
    grps, lats, lons = (lax.axis_size(name) for name in ("grp", "lat", "lon"))
    levels, lat_count, lon_local = aloft_gridpoint.shape
    block_air = heat_transfer_factors.shape[3]
    blocks = lon_local // block_air
    olev, rows, cols = marine_heat.shape
    m_local, degrees = associated_polynomial_quadrature.shape[1:]
    lon_per, lat_per = lons // grps, lats // grps
    wide = lons * LANES
    line = lat_count * BLK_PAD
    parts = 2 * levels
    n_local = degrees // lats
    width = -(-parts * m_local // LANES) * LANES
    warm_ways = skin_warmth_feeding_panels.shape[2]
    cool_ways = heat_feeding_panels.shape[2]
    vmem = pl.BlockSpec(memory_space=pltpu.VMEM)
    hbm = pl.BlockSpec(memory_space=pl.ANY)
    f32, bf16 = jnp.float32, jnp.bfloat16
    dma, dmas = pltpu.SemaphoreType.DMA, lambda n: pltpu.SemaphoreType.DMA((n,))

    aloft = aloft_gridpoint.astype(f32).reshape(levels, lat_count, blocks, block_air)
    aloft = jnp.pad(
        aloft.transpose(0, 3, 1, 2),
        ((0, 0), (0, 8 - block_air), (0, 0), (0, BLK_PAD - blocks)),
    ).reshape(levels * 8, line)
    warm_ids = jnp.pad(
        skin_warmth_feeding_panels.transpose(0, 2, 1),
        ((0, 0), (0, 0), (0, BLK_PAD - blocks)),
        constant_values=-1,
    ).reshape(lat_count, warm_ways * BLK_PAD)
    cool_ids = heat_feeding_panels.reshape(1, rows * cool_ways)

    sizes = (
        grps, lats, lons, lat_count, levels, lon_local, block_air, m_local, degrees, olev, rows, cols
    )
    spec, ocean = pl.pallas_call(
        functools.partial(step_kernel, sizes),
        out_shape=(
            jax.ShapeDtypeStruct((n_local, width), f32),
            jax.ShapeDtypeStruct((olev, rows, cols), f32),
        ),
        in_specs=[hbm] * 6 + [vmem] * 5,
        out_specs=(vmem, vmem),
        scratch_shapes=[
            pltpu.SMEM((lat_count,), jnp.int32),
            pltpu.SMEM((levels,), f32),
            pltpu.SMEM((levels,), f32),
            pltpu.VMEM((lat_count, m_local, degrees), bf16),
            pltpu.VMEM((lat_count * blocks * warm_ways, block_air, cols), bf16),
            pltpu.VMEM((rows * cool_ways, block_air, cols), bf16),
            pltpu.VMEM((lats, lon_per, rows, cols), bf16),
            pltpu.VMEM((lons, lat_per, line // 16, LANES), bf16),
            pltpu.VMEM((line, 2 * wide), bf16),
            pltpu.VMEM((lat_count * 8, 2 * wide), f32),
            pltpu.VMEM((rows, cols), bf16),
            pltpu.VMEM((line // 16, LANES), f32),
            pltpu.VMEM((grps, line // 16, LANES), f32),
            pltpu.VMEM((8, line), f32),
            pltpu.VMEM((grps, 8, line), f32),
            pltpu.VMEM((rows, cols), f32),
            pltpu.VMEM((grps, rows, cols), f32),
            pltpu.VMEM((olev + 1, rows + 16, cols + 2 * LANES), f32),
            pltpu.VMEM((lons, parts * lat_count, LANES), f32),
            pltpu.VMEM((lons, parts * lat_count, LANES), f32),
            pltpu.VMEM((lats, parts * lat_count, LANES), bf16),
            pltpu.VMEM((lats // 2, m_local, lat_count * n_local), bf16),
            pltpu.VMEM((lats, m_local, lat_count * n_local), bf16),
            pltpu.VMEM((parts * m_local, lat_count * n_local), f32),
            dmas(6),
            dma,
            dmas(lons),
            dmas(lon_per),
            dma,
            dmas(grps),
            dmas(lats),
            dmas(lat_per),
            dmas(lats),
            dmas(lats),
            dmas(lons),
            dmas(lons),
            dmas(grps),
            dmas(grps),
            dma,
            dmas(grps),
            dmas(8),
            dmas(8),
            dmas(lons),
            dmas(lons),
            dmas(lats),
            dmas(lats),
            dmas(lats // 2),
            dmas(lats),
            dmas(lats // 2),
            dmas(lats),
        ],
        compiler_params=pltpu.CompilerParams(
            collective_id=0, has_side_effects=True, vmem_limit_bytes=VMEM_LIMIT
        ),
    )(
        parallel_nodes,
        layer_pressure_share,
        layer_sensitivity,
        associated_polynomial_quadrature,
        skin_warmth_mapping_factors.reshape(-1, block_air, cols),
        heat_transfer_factors.reshape(-1, block_air, cols),
        aloft,
        marine_heat,
        water_indicator,
        warm_ids,
        cool_ids,
    )
    spectra = spec[:, : parts * m_local].reshape(n_local, parts, m_local)
    return (spectra, ocean)


def solution(mesh):
    in_specs = (
        P("grp", "lat", "lon"),
        P("lat"),
        P("grp"),
        P("grp"),
        P("lat", "lon", None),
        P("grp", "lat", "lon"),
        P("lat", "lon"),
        P("lat", "lon", None),
        P("lat", "lon", None, None, None),
        P("lat", "lon", None),
        P("lat", "lon", None, None, None),
    )
    out_specs = (P("lat", "grp", "lon"), P("grp", "lat", "lon"))
    return jax.shard_map(
        per_device, mesh=mesh, in_specs=in_specs, out_specs=out_specs, check_vma=False
    )
```

time: 499 us -> 72.9 us (0.15)
  the two profiles are of different devices: /device:TPU:6 before, /device:TPU:2 now
where the time goes in v2:
time: 72.9 us; the launch traced here: 72.6 us
  Pallas kernels  64.8 us (89%)
  local copies, waits for them, and re-layouts  7.09 us (10%)
  between operations  0.74 us (1%)
    pallas_call x1, Pallas kernels, per_device(): pl.pallas_call(functools.partial(step_kernel, sizes), out_shape=(jax.Shap...  64.8 us
    unnamed x16, local copies, waits for them, and re-layouts  4.17 us

profile of v2, /device:TPU:2, one launch (start us, length us, event | category | flops | bytes accessed | tf_op | source)
XLA Modules:
  0.0 72.6 jit_solution(18037220547279638414)
XLA Ops:
  0.6 0.7 pad.10
  1.3 0.1 reshape.33.warm_ids_ref
  1.4 0.8 %copy.24 = s32[32,1,4]{2,0,1:T(8,128)S(1)} copy(s32[32,1,4]{0,2,1:T(4,128)} %param.18) | data formatting | bytes 1024 | tf_op args[7]
  2.2 0.1 reshape.34.cool_ids_ref
  2.3 0.9 %reshape.30 = bf16[2,8,54,6]{3,2,1,0:T(8,128)(2,1)S(1)} reshape(bf16[2,8,324]{2,1,0:T(8,128)(2,1)} %param.11) | data formatting | bytes 20736 | tf_op jit(solution)/shard_map/reshape | solution.py:717
  3.2 0.2 copy.23
  3.4 0.1 reshape.37.aloft_ref
  3.5 1.0 %copy.22 = bf16[32,1,4,6,128]{4,3,2,0,1:T(8,128)(2,1)S(1)} copy(bf16[32,1,4,6,128]{4,2,3,1,0:T(4,128)(2,1)} %param.19) | data formatting | bytes 393216 | tf_op args[8]
  4.5 0.0 copy-start
  4.5 0.0 copy-start.1
  4.5 0.0 copy-start.2
  4.5 0.0 copy-start.3
  4.6 0.0 copy-start.4
  4.6 0.0 copy-start.5
  4.6 1.7 %copy.21 = bf16[8,54,2,6,128]{4,3,2,1,0:T(8,128)(2,1)S(1)} copy(bf16[8,54,2,6,128]{4,2,3,1,0:T(2,128)(2,1)} %param.21) | data formatting | bytes 2654208 | tf_op args[10]
  6.3 0.0 copy-done
  6.3 0.0 copy-done.1
  6.4 0.0 copy-done.2
  6.4 0.0 copy-done.3
  6.4 0.0 copy-done.4
  6.4 0.0 copy-done.5
  6.4 64.8 %shard_map.122 = (f32[80,384]{1,0:T(8,128)S(1)}, f32[4,32,128]{2,1,0:T(8,128)S(1)}) custom-call(s32[8]{0:T(128)S(1)} %copy-done.3, f32[2]{0:T(128)S(1)} %copy-done.4, f32[2]{0:T(128)S(1)} %copy-done.5, bf16[8,80,1280]{2,1,0:T(8,128)(2,1)S(1)} %copy-done, bf16[864,6,128]{2,1,0:T(8,128)(2,1)S(1)} %bitcast.9, bf16[128,6,128]{2,1,0:T(8,128)(2,1)S(1)} %bitcast.10, ...), custom_call_target="tpu_custom_call" | custom-call | tf_op jit(solution)/shard_map/pallas_call | solution.py:732
  71.2 0.8 %reshape.35 = f32[80,4,80]{2,1,0:T(4,128)} reshape(f32[80,320]{1,0:T(8,128)S(1)} %bitcast.11) | data formatting | bytes 204800 | tf_op jit(solution)/shard_map/reshape | solution.py:808
  72.0 0.6 copy.26
  (1 shorter events, 0.0 us)
Async XLA Ops:
  4.5 1.8 %copy-start = (bf16[8,80,1280]{2,1,0:T(8,128)(2,1)S(1)}, bf16[8,80,1280]{2,1,0:T(8,128)(2,1)}, u32[]{:S(2)}) copy-start(bf16[8,80,1280]{2,1,0:T(8,128)(2,1)} %quad_hbm.1) | copy-start | bytes 4915204
  4.5 1.8 %copy-start.1 = (f32[4,32,128]{2,1,0:T(8,128)S(1)}, f32[4,32,128]{2,1,0:T(8,128)}, u32[]{:S(2)}) copy-start(f32[4,32,128]{2,1,0:T(8,128)} %heat_ref.1) | copy-start | bytes 196612
  4.5 1.8 %copy-start.2 = (s32[32,128]{1,0:T(8,128)S(1)}, s32[32,128]{1,0:T(8,128)}, u32[]{:S(2)}) copy-start(s32[32,128]{1,0:T(8,128)} %water_ref.1) | copy-start | bytes 49156
  4.5 1.8 %copy-start.3 = (s32[8]{0:T(128)S(1)}, s32[8]{0:T(128)}, u32[]{:S(2)}) copy-start(s32[8]{0:T(128)} %nodes_hbm.1) | copy-start | bytes 100
  4.6 1.8 %copy-start.4 = (f32[2]{0:T(128)S(1)}, f32[2]{0:T(128)}, u32[]{:S(2)}) copy-start(f32[2]{0:T(128)} %share_hbm.1) | copy-start | bytes 28
  4.6 1.8 %copy-start.5 = (f32[2]{0:T(128)S(1)}, f32[2]{0:T(128)}, u32[]{:S(2)}) copy-start(f32[2]{0:T(128)} %sens_hbm.1) | copy-start | bytes 28

commit v3 on v2

--- a/solution.py
+++ b/solution.py
@@ -21,11 +21,16 @@
     return lax.rem(index + offset, count)
 
 
-def greet(partners):
+def greet(partners, sometimes, extra):
     barrier = pltpu.get_barrier_semaphore()
     for partner in partners:
         pl.semaphore_signal(barrier, inc=1, device_id=partner, device_id_type=MESH_ID)
-    pl.semaphore_wait(barrier, len(partners))
+    for needed, partner in sometimes:
+        @pl.when(needed)
+        def _(partner=partner):
+            pl.semaphore_signal(barrier, inc=1, device_id=partner, device_id_type=MESH_ID)
+
+    pl.semaphore_wait(barrier, len(partners) + extra)
 
 
 def remote(src, dst, send_sem, recv_sem, partner):
@@ -64,11 +69,11 @@
     quad_hbm,
     warm_hbm,
     cool_hbm,
-    aloft_ref,
+    aloft_raw_ref,
     heat_ref,
     water_ref,
-    warm_ids_ref,
-    cool_ids_ref,
+    warm_raw_ref,
+    cool_raw_ref,
     spec_ref,
     ocean_ref,
     nodes_ref,
@@ -81,6 +86,9 @@
     flux_ref,
     e1_ref,
     e2_ref,
+    aloft_ref,
+    warm_ids_ref,
+    cool_ids_ref,
     stage,
     part,
     gathered,
@@ -90,6 +98,7 @@
     flux_in,
     ext,
     waves,
+    waves_out,
     waves_in,
     fourier,
     quad_out,
@@ -131,8 +140,8 @@
     n_local = degrees // lats
     line = lat_count * BLK_PAD
     lon_per, lat_per = lons // grps, lats // grps
-    sea_owner, yy = y // lon_per, lax.rem(y, lon_per)
-    flux_owner, tt = t // lat_per, lax.rem(t, lat_per)
+    flux_owner, yy = y // lon_per, lax.rem(y, lon_per)
+    sea_owner, tt = t // lat_per, lax.rem(t, lat_per)
     core = lax.rem(g, 2)
     sibling = {"grp": g + 1 - 2 * core}
     north, south = shifted(t, lats - 1, lats), shifted(t, 1, lats)
@@ -152,7 +161,6 @@
         ({"lat": north, "lon": west}, first_rows, high_rows, high_cols),
     ]
     pairs = lats // 2
-    early = 5 * pairs // 8
 
     fetches = [
         pltpu.make_async_copy(src, dst, local_sems.at[k])
@@ -171,67 +179,37 @@
         fetch.start()
 
     stage[...] = heat_ref[0].astype(bf16)
-    for level in range(olev):
-        ext[level, mid_rows, mid_cols] = heat_ref[level]
-    wet_mid = water_ref[...].astype(f32)
-    ext[olev, mid_rows, mid_cols] = wet_mid
-
-    for fetch in fetches[:3]:
-        fetch.wait()
-    lane = lax.broadcasted_iota(i32, (8, line), 1)
-    slot = lax.broadcasted_iota(i32, (8, line), 0)
-    block = lane % BLK_PAD
-    limit = jnp.zeros((8, line), i32)
-    for i in range(lat_count):
-        limit = jnp.where(lane // BLK_PAD == i, nodes_ref[i], limit)
-    live = (block < blocks) & (slot < block_air)
-    live = live & (y * lon_local + block * block_air + slot < limit)
-    flux_sum = share_ref[0] * aloft_ref[0:8, :]
-    for l in range(1, levels):
-        flux_sum = flux_sum + share_ref[l] * aloft_ref[8 * l : 8 * l + 8, :]
-    flux_sum = jnp.where(live, flux_sum, 0.0)
-    tiles = line // LANES
-    for k in range(tiles):
-        part[8 * k : 8 * k + 8, :] = flux_sum[:, k * LANES : (k + 1) * LANES]
-
+    expected = jnp.where(g == 0, jnp.where(sea_owner == 0, lats - 1, lats), 0)
+    keepers = [(g * lat_per + k, {"grp": jnp.int32(0), "lat": g * lat_per + k}) for k in range(lat_per)]
     greet(
         [{"grp": shifted(g, d, grps)} for d in range(1, grps)]
         + [{"lon": shifted(y, d, lons)} for d in range(1, lons)]
         + [{"lat": shifted(t, d, lats)} for d in range(1, lats)]
-        + [
-            {"grp": shifted(g, d, grps), "lon": shifted(y, e, lons)}
-            for d in range(1, grps)
-            for e in range(1, lons)
-        ]
-        + [partner for partner, _, _, _ in halo[4:]]
+        + [partner for partner, _, _, _ in halo[4:]],
+        [((g != 0) | (at != t), partner) for at, partner in keepers],
+        expected,
     )
 
     @pl.when(g == 0)
     def _():
-        for d in range(1, lons):
+        for d in range(1, lats):
             remote(
                 stage,
-                sea_ref.at[t, yy],
+                sea_ref.at[y, tt],
                 sea1_send.at[d],
-                sea1_recv.at[yy],
-                {"grp": sea_owner, "lon": shifted(y, d, lons)},
+                sea1_recv.at[tt],
+                {"grp": sea_owner, "lat": shifted(t, d, lats)},
             ).start()
 
     @pl.when((g == 0) & (sea_owner != 0))
     def _():
         remote(
-            stage, sea_ref.at[t, yy], sea1_send.at[0], sea1_recv.at[yy], {"grp": sea_owner}
+            stage, sea_ref.at[y, tt], sea1_send.at[0], sea1_recv.at[tt], {"grp": sea_owner}
         ).start()
 
     @pl.when((g == 0) & (sea_owner == 0))
     def _():
-        sea_ref[t, yy] = stage[...]
-
-    @pl.when(g != flux_owner)
-    def _():
-        remote(
-            part, gathered.at[g], flux0_send, flux0_recv.at[g], {"grp": flux_owner}
-        ).start()
+        sea_ref[y, tt] = stage[...]
 
     def offset_of(rank):
         half = jnp.where(rank % 2 == 1, (rank + 1) // 2, pairs - rank // 2)
@@ -286,41 +264,98 @@
 
         return carry
 
+    def source(rank):
+        return shifted(t, lats - offset_of(rank), lats)
+
+    def pass_on(rank, carry):
+        @pl.when((rank == 0) & (core == 0))
+        def _():
+            own_copy.wait()
+
+        @pl.when((rank != 0) | (core != 0))
+        def _():
+            landed(quad_in.at[source(rank)], quad_recv.at[source(rank)])
+
+        remote(
+            quad_in.at[source(rank)],
+            quad_in.at[source(rank)],
+            pass_send.at[rank],
+            pass_recv.at[source(rank)],
+            sibling,
+        ).start()
+        return carry
+
     fetches[3].wait()
-    lax.fori_loop(0, early, pack_and_send, 0)
-
-    for k in range(lon_per):
-        @pl.when((g != 0) | (lon_per * g + k != y))
+    lax.fori_loop(0, pairs, pack_and_send, 0)
+
+    for fetch in fetches[:3]:
+        fetch.wait()
+    tiles = line // LANES
+    raw = jnp.concatenate([aloft_raw_ref[l].astype(f32) for l in range(levels)], axis=0)
+    source_id = lax.broadcasted_iota(i32, (lon_local, 8 * BLK_PAD), 0)
+    target_id = lax.broadcasted_iota(i32, (lon_local, 8 * BLK_PAD), 1)
+    target_block, target_slot = target_id % BLK_PAD, target_id // BLK_PAD
+    sorting = jnp.where(
+        (target_block < blocks)
+        & (target_slot < block_air)
+        & (source_id == target_block * block_air + target_slot),
+        1.0,
+        0.0,
+    ).astype(bf16)
+    by_slot = jnp.dot(raw.astype(bf16), sorting, preferred_element_type=f32)
+    aloft_ref[...] = jnp.zeros_like(aloft_ref)
+    out_lane = lax.broadcasted_iota(i32, (8, LANES), 1)
+    out_row = lax.broadcasted_iota(i32, (8, LANES), 0)
+    for l in range(levels):
+        for q in range(block_air):
+            k = q // 2
+            two = by_slot[8 * l : 8 * l + 8, k * LANES : (k + 1) * LANES]
+            other = pltpu.roll(two, BLK_PAD, 1)
+            both = jnp.where((out_lane < BLK_PAD) == (q % 2 == 0), two, other)
+            for k in range(tiles):
+                mine = out_row == 2 * k + out_lane // BLK_PAD
+                aloft_ref[8 * l + q : 8 * l + q + 1, k * LANES : (k + 1) * LANES] = jnp.sum(
+                    jnp.where(mine, both, 0.0), axis=0, keepdims=True
+                )
+    lane = lax.broadcasted_iota(i32, (8, line), 1)
+    slot = lax.broadcasted_iota(i32, (8, line), 0)
+    block = lane % BLK_PAD
+    limit = jnp.zeros((8, line), i32)
+    for i in range(lat_count):
+        limit = jnp.where(lane // BLK_PAD == i, nodes_ref[i], limit)
+    live = (block < blocks) & (slot < block_air)
+    live = live & (y * lon_local + block * block_air + slot < limit)
+    flux_sum = share_ref[0] * aloft_ref[0:8, :]
+    for l in range(1, levels):
+        flux_sum = flux_sum + share_ref[l] * aloft_ref[8 * l : 8 * l + 8, :]
+    flux_sum = jnp.where(live, flux_sum, 0.0)
+    for k in range(tiles):
+        part[8 * k : 8 * k + 8, :] = flux_sum[:, k * LANES : (k + 1) * LANES]
+
+    @pl.when(g != flux_owner)
+    def _():
+        remote(
+            part, gathered.at[g], flux0_send, flux0_recv.at[g], {"grp": flux_owner}
+        ).start()
+
+    for k in range(lat_per):
+        @pl.when((g != 0) | (lat_per * g + k != t))
         def _():
-            landed(sea_ref.at[t, k], sea1_recv.at[k])
-
-    for d in range(1, lats):
+            landed(sea_ref.at[y, k], sea1_recv.at[k])
+
+    for d in range(1, lons):
         remote(
-            sea_ref.at[t],
-            sea_ref.at[t],
+            sea_ref.at[y],
+            sea_ref.at[y],
             sea2_send.at[d],
-            sea2_recv.at[t],
-            {"lat": shifted(t, d, lats)},
+            sea2_recv.at[y],
+            {"lon": shifted(y, d, lons)},
         ).start()
 
-    @pl.when(g == flux_owner)
-    def _():
-        gathered[g] = part[...]
-        for d in range(1, grps):
-            other = shifted(g, d, grps)
-            landed(gathered.at[other], flux0_recv.at[other])
-        total = gathered[0]
-        for other in range(1, grps):
-            total = total + gathered[other]
-        flux_ref[y, tt] = total.astype(bf16)
-        for d in range(1, lats):
-            remote(
-                flux_ref.at[y, tt],
-                flux_ref.at[y, tt],
-                flux1_send.at[d],
-                flux1_recv.at[tt],
-                {"lat": shifted(t, d, lats)},
-            ).start()
+    for level in range(olev):
+        ext[level, mid_rows, mid_cols] = heat_ref[level]
+    wet_mid = water_ref[...].astype(f32)
+    ext[olev, mid_rows, mid_cols] = wet_mid
 
     def tables(i, carry):
         count = jnp.full((8, LANES), nodes_ref[i], i32).astype(f32)
@@ -351,42 +386,67 @@
 
     lax.fori_loop(0, lat_count // 2, tables, 0)
 
-    for k in range(lat_per):
-        @pl.when(g * lat_per + k != t)
+    @pl.when(g == flux_owner)
+    def _():
+        gathered[g] = part[...]
+        for d in range(1, grps):
+            other = shifted(g, d, grps)
+            landed(gathered.at[other], flux0_recv.at[other])
+        total = gathered[0]
+        for other in range(1, grps):
+            total = total + gathered[other]
+        flux_ref[t, yy] = total.astype(bf16)
+        for d in range(1, lons):
+            remote(
+                flux_ref.at[t, yy],
+                flux_ref.at[t, yy],
+                flux1_send.at[d],
+                flux1_recv.at[yy],
+                {"lon": shifted(y, d, lons)},
+            ).start()
+
+    lax.fori_loop(lat_count // 2, lat_count, tables, 0)
+
+    for k in range(lon_per):
+        @pl.when(g * lon_per + k != y)
         def _():
-            landed(flux_ref.at[y, k], flux1_recv.at[k])
+            landed(flux_ref.at[t, k], flux1_recv.at[k])
+
+    for d in range(1, lats):
+        remote(
+            flux_ref.at[t],
+            flux_ref.at[t],
+            flux2_send.at[d],
+            flux2_recv.at[t],
+            {"lat": shifted(t, d, lats)},
+        ).start()
 
     for d in range(1, lons):
-        remote(
-            flux_ref.at[y],
-            flux_ref.at[y],
-            flux2_send.at[d],
-            flux2_recv.at[y],
-            {"lon": shifted(y, d, lons)},
-        ).start()
-
-    lax.fori_loop(lat_count // 2, lat_count, tables, 0)
-
-    for d in range(1, lats):
-        other = shifted(t, d, lats)
+        other = shifted(y, d, lons)
         landed(sea_ref.at[other], sea2_recv.at[other])
 
-    count_rows = lats * lon_per * rows
+    count_rows = lons * lat_per * rows
     table = sea_ref[...].reshape(count_rows, cols).astype(f32)
     table = jnp.concatenate(
         [jnp.transpose(table[k : k + LANES]) for k in range(0, count_rows, LANES)], axis=1
     ).astype(bf16)
     picks = 2 * blocks
+    warm_ids_ref[...] = jnp.full_like(warm_ids_ref, -1)
+    for i in range(lat_count):
+        for k in range(warm_raw_ref.shape[1]):
+            warm_ids_ref[i : i + 1, k * BLK_PAD : k * BLK_PAD + blocks] = warm_raw_ref[
+                i, k : k + 1, :
+            ]
     chosen = warm_ids_ref[...]
     column, row = chosen % lons, chosen // lons
-    spot = (row // rows) * (lon_per * rows) + (column % lon_per) * rows + row % rows
-    spot = jnp.where((column // lon_per == g) & (chosen >= 0), spot, -1)
+    band = row // rows
+    spot = (column * lat_per + band % lat_per) * rows + row % rows
+    spot = jnp.where((band // lat_per == g) & (chosen >= 0), spot, -1)
     fetches[5].wait()
     table_row = lax.broadcasted_iota(i32, (count_rows, LANES), 0)
     pick_id = lax.broadcasted_iota(i32, (picks, 8, LANES), 0)
     pick_lane = lax.broadcasted_iota(i32, (picks, 8, LANES), 2)
     diagonal = pick_lane == (pick_id % 2) * BLK_PAD + pick_id // 2
-    out_lane = lax.broadcasted_iota(i32, (8, LANES), 1)
     fill = jnp.zeros((picks, 8 - block_air, LANES), f32)
     warm_sums = []
     for i in range(lat_count):
@@ -409,59 +469,6 @@
             warmth_send.at[d],
             warmth_recv.at[g],
             {"grp": shifted(g, d, grps)},
-        ).start()
-
-    lax.fori_loop(early, pairs, pack_and_send, 0)
-
-    for d in range(1, lons):
-        other = shifted(y, d, lons)
-        landed(flux_ref.at[other], flux2_recv.at[other])
-    chosen = cool_ids_ref[0:1, :]
-    parallel, place = chosen // (blocks * lons), chosen % (blocks * lons)
-    band, within = parallel // lat_count, parallel % lat_count
-    lon, blk = place // blocks, place % blocks
-    group = (lon * lat_per + band % lat_per) * tiles + within // 2
-    group = jnp.where(band // lat_per == g, group, -1)
-    spot = (within % 2) * BLK_PAD + blk
-    group_count = lons * lat_per * tiles
-    one_hot = jnp.where(
-        lax.broadcasted_iota(i32, (LANES, LANES), 0) == spot, 1.0, 0.0
-    ).astype(bf16)
-    found = jnp.dot(
-        flux_ref[...].reshape(group_count * 8, LANES), one_hot, preferred_element_type=f32
-    ).reshape(group_count, 8, LANES)
-    group_id = lax.broadcasted_iota(i32, (group_count, 8, LANES), 0)
-    air = jnp.sum(jnp.where(group_id == group[None], found, 0.0), axis=0)
-    width = LANES * 8
-    repeat = jnp.where(
-        lax.broadcasted_iota(i32, (LANES, width), 0)
-        == lax.broadcasted_iota(i32, (LANES, width), 1) // 8,
-        1.0,
-        0.0,
-    ).astype(bf16)
-    air = jnp.dot(air.astype(bf16), repeat, preferred_element_type=f32)
-    own_slot = lax.broadcasted_iota(i32, (8, width), 1) % 8 == lax.broadcasted_iota(
-        i32, (8, width), 0
-    )
-    air = jnp.sum(jnp.where(own_slot, air, 0.0), axis=0, keepdims=True)
-    per_row = width // rows
-    air = jnp.where(
-        lax.broadcasted_iota(i32, (rows, width), 1) // per_row
-        == lax.broadcasted_iota(i32, (rows, width), 0),
-        air,
-        0.0,
-    ).astype(bf16)
-    fetches[4].wait()
-    factor = cool_ref[...].astype(f32)
-    factor = jnp.concatenate(
-        [factor, jnp.zeros((LANES, 8 - block_air, LANES), f32)], axis=1
-    ).reshape(width, LANES)
-    flux_out[...] = jnp.dot(air, factor.astype(bf16), preferred_element_type=f32)
-
-    @pl.when(g != 0)
-    def _():
-        remote(
-            flux_out, flux_in.at[g], fluxp_send, fluxp_recv.at[g], {"grp": jnp.int32(0)}
         ).start()
 
     warmth_in[g] = warmth_out[...]
@@ -497,11 +504,100 @@
                 for k in range(lons):
                     waves[k, row : row + 1, :] = out[:, k * LANES : (k + 1) * LANES]
 
+    waves_out[...] = waves[...].astype(bf16)
     for d in range(1, lons):
         other = shifted(y, d, lons)
         remote(
-            waves.at[other], waves_in.at[y], waves_send.at[d], waves_recv.at[y], {"lon": other}
+            waves_out.at[other],
+            waves_in.at[y],
+            waves_send.at[d],
+            waves_recv.at[y],
+            {"lon": other},
         ).start()
+
+    for d in range(1, lats):
+        other = shifted(t, d, lats)
+        landed(flux_ref.at[other], flux2_recv.at[other])
+    ways = cool_raw_ref.shape[0]
+    for k in range(ways):
+        cool_ids_ref[0:1, k * rows : (k + 1) * rows] = cool_raw_ref[k : k + 1, :]
+    chosen = cool_ids_ref[0:1, :]
+    parallel, place = chosen // (blocks * lons), chosen % (blocks * lons)
+    band, within = parallel // lat_count, parallel % lat_count
+    lon, blk = place // blocks, place % blocks
+    group = (band * lon_per + lon % lon_per) * tiles + within // 2
+    group = jnp.where(lon // lon_per == g, group, -1)
+    spot = (within % 2) * BLK_PAD + blk
+    group_count = lats * lon_per * tiles
+    one_hot = jnp.where(
+        lax.broadcasted_iota(i32, (LANES, LANES), 0) == spot, 1.0, 0.0
+    ).astype(bf16)
+    found = jnp.dot(
+        flux_ref[...].reshape(group_count * 8, LANES), one_hot, preferred_element_type=f32
+    ).reshape(group_count, 8, LANES)
+    group_id = lax.broadcasted_iota(i32, (group_count, 8, LANES), 0)
+    air = jnp.sum(jnp.where(group_id == group[None], found, 0.0), axis=0)
+    width = rows * block_air * 8
+    to = lax.broadcasted_iota(i32, (LANES, width), 1)
+    repeat = jnp.where(
+        (to % 8 < ways)
+        & (lax.broadcasted_iota(i32, (LANES, width), 0) == (to % 8) * rows + to // (8 * block_air)),
+        1.0,
+        0.0,
+    ).astype(bf16)
+    air = jnp.dot(air.astype(bf16), repeat, preferred_element_type=f32)
+    to = lax.broadcasted_iota(i32, (8, width), 1)
+    own_slot = (to // 8) % block_air == lax.broadcasted_iota(i32, (8, width), 0)
+    air = jnp.sum(jnp.where(own_slot, air, 0.0), axis=0, keepdims=True)
+    air = jnp.where(
+        lax.broadcasted_iota(i32, (rows, width), 1) // (8 * block_air)
+        == lax.broadcasted_iota(i32, (rows, width), 0),
+        air,
+        0.0,
+    ).astype(bf16)
+    fetches[4].wait()
+    factor = cool_ref[...].astype(f32)
+    factor = jnp.concatenate(
+        [factor, jnp.zeros((rows * block_air, 8 - ways, LANES), f32)], axis=1
+    ).reshape(width, LANES)
+    flux_out[...] = jnp.dot(air, factor.astype(bf16), preferred_element_type=f32)
+
+    @pl.when(g != 0)
+    def _():
+        remote(
+            flux_out, flux_in.at[g], fluxp_send, fluxp_recv.at[g], {"grp": jnp.int32(0)}
+        ).start()
+
+    lax.fori_loop(0, pairs // 2, pass_on, 0)
+
+    total = waves[y]
+    for d in range(1, lons):
+        other = shifted(y, d, lons)
+        landed(waves_in.at[other], waves_recv.at[other])
+        total = total + waves_in[other].astype(f32)
+    fourier[t] = total.astype(bf16)
+
+    def send_fourier(offset):
+        @pl.when(offset != 0)
+        def _():
+            remote(
+                fourier.at[t],
+                fourier.at[t],
+                fourier_send.at[offset],
+                fourier_recv.at[t],
+                {"lat": shifted(t, offset, lats)},
+            ).start()
+
+    def send_near(rank, carry):
+        send_fourier(offset_of(rank))
+        return carry
+
+    def send_far(rank, carry):
+        send_fourier(offset_of(rank) + 1 - 2 * core)
+        return carry
+
+    lax.fori_loop(0, pairs, send_near, 0)
+    lax.fori_loop(0, pairs, send_far, 0)
 
     @pl.when(g == 0)
     def _():
@@ -520,45 +616,46 @@
             partner,
         ).start()
 
-    waves_in[y] = waves[y]
-    for d in range(1, lons):
-        other = shifted(y, d, lons)
-        landed(waves_in.at[other], waves_recv.at[other])
-    total = waves_in[0]
-    for other in range(1, lons):
-        total = total + waves_in[other]
-    fourier[t] = total.astype(bf16)
-    for d in range(1, lats):
-        remote(
-            fourier.at[t],
-            fourier.at[t],
-            fourier_send.at[d],
-            fourier_recv.at[t],
-            {"lat": shifted(t, d, lats)},
-        ).start()
-
-    def source(rank):
-        return shifted(t, lats - offset_of(rank), lats)
-
-    def pass_on(rank, carry):
-        @pl.when((rank == 0) & (core == 0))
+    lax.fori_loop(pairs // 2, pairs, pass_on, 0)
+
+    span = lat_count * n_local
+    repeat_row = lax.broadcasted_iota(i32, (LANES, span), 0)
+    repeat = jnp.where(
+        (repeat_row < parts * lat_count)
+        & (repeat_row % lat_count == lax.broadcasted_iota(i32, (LANES, span), 1) // n_local),
+        1.0,
+        0.0,
+    ).astype(bf16)
+    fill = jnp.zeros((LANES - parts * lat_count, LANES), f32)
+    part_lane = lax.broadcasted_iota(i32, (m_local, LANES), 1) // lat_count
+    sums[...] = jnp.zeros_like(sums)
+
+    def add_source(s):
+        @pl.when(s != t)
         def _():
-            own_copy.wait()
-
-        @pl.when((rank != 0) | (core != 0))
-        def _():
-            landed(quad_in.at[source(rank)], quad_recv.at[source(rank)])
-
-        remote(
-            quad_in.at[source(rank)],
-            quad_in.at[source(rank)],
-            pass_send.at[rank],
-            pass_recv.at[source(rank)],
-            sibling,
-        ).start()
+            landed(fourier.at[s], fourier_recv.at[s])
+
+        columns = jnp.transpose(jnp.concatenate([fourier[s].astype(f32), fill], axis=0))[:m_local]
+        own = jnp.concatenate(
+            [jnp.where(part_lane == a, columns, 0.0) for a in range(parts)], axis=0
+        ).astype(bf16)
+        coef = jnp.dot(own, repeat, preferred_element_type=f32)
+        quad = quad_in[s].astype(f32)
+        for a in range(parts):
+            at = slice(a * m_local, (a + 1) * m_local)
+            sums[at, :] = sums[at, :] + coef[at] * quad
+
+    def add_direct(rank, carry):
+        add_source(source(rank))
         return carry
 
-    lax.fori_loop(0, pairs, pass_on, 0)
+    def add_passed(rank, carry):
+        s = shifted(source(rank), lats - 1 + 2 * core, lats)
+        landed(quad_in.at[s], pass_recv.at[s])
+        add_source(s)
+        return carry
+
+    lax.fori_loop(0, pairs, add_direct, 0)
 
     for index, (partner, src_rows, dst_rows, dst_cols) in enumerate(halo):
         landed(ext.at[:, dst_rows, dst_cols], halo_recv.at[index])
@@ -578,46 +675,6 @@
             field = field + KAPPA * wet * total
         ocean_ref[level] = field[mid_rows, mid_cols]
 
-    for d in range(1, lats):
-        other = shifted(t, d, lats)
-        landed(fourier.at[other], fourier_recv.at[other])
-    coefs = [fourier[k].astype(f32) for k in range(lats)]
-    columns = []
-    for a in range(parts):
-        tall = jnp.concatenate(
-            [coef[a * lat_count : (a + 1) * lat_count] for coef in coefs], axis=0
-        )
-        columns.append(jnp.transpose(tall)[:m_local])
-    columns = jnp.concatenate(columns, axis=0)
-    span = lat_count * n_local
-    repeat = jnp.where(
-        lax.broadcasted_iota(i32, (lats * lat_count, span), 0) % lat_count
-        == lax.broadcasted_iota(i32, (lats * lat_count, span), 1) // n_local,
-        1.0,
-        0.0,
-    ).astype(bf16)
-    lane = lax.broadcasted_iota(i32, columns.shape, 1)
-    sums[...] = jnp.zeros_like(sums)
-
-    def add_source(s):
-        own = jnp.where(lane // lat_count == s, columns, 0.0).astype(bf16)
-        coef = jnp.dot(own, repeat, preferred_element_type=f32)
-        quad = quad_in[s].astype(f32)
-        for a in range(parts):
-            at = slice(a * m_local, (a + 1) * m_local)
-            sums[at, :] = sums[at, :] + coef[at] * quad
-
-    def add_direct(rank, carry):
-        add_source(source(rank))
-        return carry
-
-    def add_passed(rank, carry):
-        s = shifted(source(rank), lats - 1 + 2 * core, lats)
-        landed(quad_in.at[s], pass_recv.at[s])
-        add_source(s)
-        return carry
-
-    lax.fori_loop(0, pairs, add_direct, 0)
     lax.fori_loop(0, pairs, add_passed, 0)
 
     folded = jnp.zeros((parts * m_local, LANES), f32)
@@ -640,32 +697,32 @@
 
     @pl.when(g == 0)
     def _():
+        for d in range(1, lats):
+            landed(stage, sea1_send.at[d])
+
+    @pl.when((g == 0) & (sea_owner != 0))
+    def _():
+        landed(stage, sea1_send.at[0])
+
+    @pl.when(g != flux_owner)
+    def _():
+        landed(part, flux0_send)
+
+    @pl.when(g == flux_owner)
+    def _():
         for d in range(1, lons):
-            landed(stage, sea1_send.at[d])
-
-    @pl.when((g == 0) & (sea_owner != 0))
-    def _():
-        landed(stage, sea1_send.at[0])
-
-    @pl.when(g != flux_owner)
-    def _():
-        landed(part, flux0_send)
-
-    @pl.when(g == flux_owner)
-    def _():
-        for d in range(1, lats):
-            landed(flux_ref.at[y, tt], flux1_send.at[d])
+            landed(flux_ref.at[t, yy], flux1_send.at[d])
 
     @pl.when(g != 0)
     def _():
         landed(flux_out, fluxp_send)
 
     for d in range(1, lats):
-        landed(sea_ref.at[t], sea2_send.at[d])
+        landed(flux_ref.at[t], flux2_send.at[d])
         landed(fourier.at[t], fourier_send.at[d])
     for d in range(1, lons):
-        landed(flux_ref.at[y], flux2_send.at[d])
-        landed(waves.at[0], waves_send.at[d])
+        landed(sea_ref.at[y], sea2_send.at[d])
+        landed(waves_out.at[0], waves_send.at[d])
     for d in range(1, grps):
         landed(warmth_out, warmth_send.at[d])
     for index, (partner, src_rows, dst_rows, dst_cols) in enumerate(halo):
@@ -714,17 +771,9 @@
     f32, bf16 = jnp.float32, jnp.bfloat16
     dma, dmas = pltpu.SemaphoreType.DMA, lambda n: pltpu.SemaphoreType.DMA((n,))
 
-    aloft = aloft_gridpoint.astype(f32).reshape(levels, lat_count, blocks, block_air)
-    aloft = jnp.pad(
-        aloft.transpose(0, 3, 1, 2),
-        ((0, 0), (0, 8 - block_air), (0, 0), (0, BLK_PAD - blocks)),
-    ).reshape(levels * 8, line)
-    warm_ids = jnp.pad(
-        skin_warmth_feeding_panels.transpose(0, 2, 1),
-        ((0, 0), (0, 0), (0, BLK_PAD - blocks)),
-        constant_values=-1,
-    ).reshape(lat_count, warm_ways * BLK_PAD)
-    cool_ids = heat_feeding_panels.reshape(1, rows * cool_ways)
+    warm_ids = skin_warmth_feeding_panels.transpose(0, 2, 1)
+    cool_ids = heat_feeding_panels[:, 0, :].transpose(1, 0)
+    cool_factors = heat_transfer_factors.transpose(0, 1, 3, 2, 4)
 
     sizes = (
         grps, lats, lons, lat_count, levels, lon_local, block_air, m_local, degrees, olev, rows, cols
@@ -743,11 +792,14 @@
             pltpu.SMEM((levels,), f32),
             pltpu.VMEM((lat_count, m_local, degrees), bf16),
             pltpu.VMEM((lat_count * blocks * warm_ways, block_air, cols), bf16),
-            pltpu.VMEM((rows * cool_ways, block_air, cols), bf16),
-            pltpu.VMEM((lats, lon_per, rows, cols), bf16),
-            pltpu.VMEM((lons, lat_per, line // 16, LANES), bf16),
+            pltpu.VMEM((rows * block_air, cool_ways, cols), bf16),
+            pltpu.VMEM((lons, lat_per, rows, cols), bf16),
+            pltpu.VMEM((lats, lon_per, line // 16, LANES), bf16),
             pltpu.VMEM((line, 2 * wide), bf16),
             pltpu.VMEM((lat_count * 8, 2 * wide), f32),
+            pltpu.VMEM((levels * 8, line), f32),
+            pltpu.VMEM((lat_count, warm_ways * BLK_PAD), jnp.int32),
+            pltpu.VMEM((8, rows * cool_ways), jnp.int32),
             pltpu.VMEM((rows, cols), bf16),
             pltpu.VMEM((line // 16, LANES), f32),
             pltpu.VMEM((grps, line // 16, LANES), f32),
@@ -757,23 +809,24 @@
             pltpu.VMEM((grps, rows, cols), f32),
             pltpu.VMEM((olev + 1, rows + 16, cols + 2 * LANES), f32),
             pltpu.VMEM((lons, parts * lat_count, LANES), f32),
-            pltpu.VMEM((lons, parts * lat_count, LANES), f32),
+            pltpu.VMEM((lons, parts * lat_count, LANES), bf16),
+            pltpu.VMEM((lons, parts * lat_count, LANES), bf16),
             pltpu.VMEM((lats, parts * lat_count, LANES), bf16),
             pltpu.VMEM((lats // 2, m_local, lat_count * n_local), bf16),
             pltpu.VMEM((lats, m_local, lat_count * n_local), bf16),
             pltpu.VMEM((parts * m_local, lat_count * n_local), f32),
             dmas(6),
             dma,
+            dmas(lats),
+            dmas(lat_per),
+            dma,
+            dmas(grps),
             dmas(lons),
             dmas(lon_per),
-            dma,
-            dmas(grps),
-            dmas(lats),
-            dmas(lat_per),
+            dmas(lons),
+            dmas(lons),
             dmas(lats),
             dmas(lats),
-            dmas(lons),
-            dmas(lons),
             dmas(grps),
             dmas(grps),
             dma,
@@ -798,8 +851,8 @@
         layer_sensitivity,
         associated_polynomial_quadrature,
         skin_warmth_mapping_factors.reshape(-1, block_air, cols),
-        heat_transfer_factors.reshape(-1, block_air, cols),
-        aloft,
+        cool_factors.reshape(-1, cool_ways, cols),
+        aloft_gridpoint,
         marine_heat,
         water_indicator,
         warm_ids,

time: 72.9 us -> 62 us (0.85)
  the two profiles are of different devices: /device:TPU:2 before, /device:TPU:122 now
where the time goes in v3:
time: 62 us; the launch traced here: 61.9 us
  Pallas kernels  57.8 us (93%)
  local copies, waits for them, and re-layouts  3.36 us (5%)
  between operations  0.77 us (1%)
    pallas_call x1, Pallas kernels, per_device(): pl.pallas_call(functools.partial(step_kernel, sizes), out_shape=(jax.Shap...  57.8 us
    unnamed x22, local copies, waits for them, and re-layouts  2.55 us

profile of v3, /device:TPU:122, one launch (start us, length us, event | category | flops | bytes accessed | tf_op | source)
XLA Modules:
  0.0 61.9 jit_solution(10497732695789317179)
XLA Ops:
  0.6 0.0 copy-start.5
  0.6 0.0 copy-start.1
  0.7 0.0 copy-start.6
  0.7 0.0 copy-start.3
  0.7 0.0 copy-start.2
  0.7 0.0 copy-start
  0.7 0.0 copy-start.9
  0.7 0.0 copy-start.8
  0.7 0.0 copy-start.7
  0.7 0.0 copy-start.4
  0.7 1.8 %copy.13 = bf16[8,54,2,6,128]{4,3,2,1,0:T(8,128)(2,1)S(1)} copy(bf16[8,54,2,6,128]{4,2,3,1,0:T(2,128)(2,1)} %param.21) | data formatting | bytes 2654208 | tf_op args[10]
  2.5 0.0 copy-done.5
  2.5 0.0 copy-done.1
  2.5 0.0 copy-done.6
  2.5 0.0 copy-done.3
  2.5 0.0 copy-done.2
  2.5 0.1 copy-done
  2.7 0.0 copy-done.9
  2.7 0.0 copy-done.8
  2.7 0.0 copy-done.7
  2.7 0.0 copy-done.4
  2.7 57.8 %shard_map.122 = (f32[80,384]{1,0:T(8,128)S(1)}, f32[4,32,128]{2,1,0:T(8,128)S(1)}) custom-call(s32[8]{0:T(128)S(1)} %copy-done.7, f32[2]{0:T(128)S(1)} %copy-done.8, f32[2]{0:T(128)S(1)} %copy-done.9, bf16[8,80,1280]{2,1,0:T(8,128)(2,1)S(1)} %copy-done, bf16[864,6,128]{2,1,0:T(8,128)(2,1)S(1)} %bitcast.9, bf16[192,4,128]{2,1,0:T(4,128)(2,1)S(1)} %bitcast.10, ...), custom_call_target="tpu_custom_call" | custom-call | tf_op jit(solution)/shard_map/pallas_call | solution.py:781
  60.5 0.8 %reshape.15 = f32[80,4,80]{2,1,0:T(4,128)} reshape(f32[80,320]{1,0:T(8,128)S(1)} %bitcast.11) | data formatting | bytes 204800 | tf_op jit(solution)/shard_map/reshape | solution.py:861
  61.3 0.6 %copy.15 = f32[4,32,128]{2,1,0:T(8,128)} copy(f32[4,32,128]{2,1,0:T(8,128)S(1)} %get-tuple-element.9) | data formatting | bytes 131072
Async XLA Ops:
  0.6 1.9 %copy-start.5 = (s32[8,54,2]{1,2,0:T(2,128)S(1)}, s32[8,54,2]{1,2,0:T(2,128)}, u32[]{:S(2)}) copy-start(s32[8,54,2]{1,2,0:T(2,128)} %param.20) | copy-start | bytes 10372
  0.6 1.9 %copy-start.1 = (bf16[32,1,4,6,128]{4,2,3,1,0:T(4,128)(2,1)S(1)}, bf16[32,1,4,6,128]{4,2,3,1,0:T(4,128)(2,1)}, u32[]{:S(2)}) copy-start(bf16[32,1,4,6,128]{4,2,3,1,0:T(4,128)(2,1)} %param.19) | copy-start | bytes 589828
  0.7 1.9 %copy-start.6 = (s32[32,1,4]{0,2,1:T(4,128)S(1)}, s32[32,1,4]{0,2,1:T(4,128)}, u32[]{:S(2)}) copy-start(s32[32,1,4]{0,2,1:T(4,128)} %param.18) | copy-start | bytes 1540
  0.7 1.9 %copy-start.3 = (s32[32,128]{1,0:T(8,128)S(1)}, s32[32,128]{1,0:T(8,128)}, u32[]{:S(2)}) copy-start(s32[32,128]{1,0:T(8,128)} %water_ref.1) | copy-start | bytes 49156
  0.7 1.9 %copy-start.2 = (f32[4,32,128]{2,1,0:T(8,128)S(1)}, f32[4,32,128]{2,1,0:T(8,128)}, u32[]{:S(2)}) copy-start(f32[4,32,128]{2,1,0:T(8,128)} %heat_ref.1) | copy-start | bytes 196612
  0.7 2.0 %copy-start = (bf16[8,80,1280]{2,1,0:T(8,128)(2,1)S(1)}, bf16[8,80,1280]{2,1,0:T(8,128)(2,1)}, u32[]{:S(2)}) copy-start(bf16[8,80,1280]{2,1,0:T(8,128)(2,1)} %quad_hbm.1) | copy-start | bytes 4915204
  0.7 2.0 %copy-start.9 = (f32[2]{0:T(128)S(1)}, f32[2]{0:T(128)}, u32[]{:S(2)}) copy-start(f32[2]{0:T(128)} %sens_hbm.1) | copy-start | bytes 28
  0.7 2.0 %copy-start.8 = (f32[2]{0:T(128)S(1)}, f32[2]{0:T(128)}, u32[]{:S(2)}) copy-start(f32[2]{0:T(128)} %share_hbm.1) | copy-start | bytes 28
  0.7 2.0 %copy-start.7 = (s32[8]{0:T(128)S(1)}, s32[8]{0:T(128)}, u32[]{:S(2)}) copy-start(s32[8]{0:T(128)} %nodes_hbm.1) | copy-start | bytes 100
  0.7 2.0 %copy-start.4 = (bf16[2,8,324]{2,1,0:T(8,128)(2,1)S(1)}, bf16[2,8,324]{2,1,0:T(8,128)(2,1)}, u32[]{:S(2)}) copy-start(bf16[2,8,324]{2,1,0:T(8,128)(2,1)} %aloft_raw_ref.1) | copy-start | bytes 31108

commit v4 on v3

--- a/solution.py
+++ b/solution.py
@@ -30,7 +30,7 @@
         def _(partner=partner):
             pl.semaphore_signal(barrier, inc=1, device_id=partner, device_id_type=MESH_ID)
 
-    pl.semaphore_wait(barrier, len(partners) + extra)
+    return len(partners) + extra
 
 
 def remote(src, dst, send_sem, recv_sem, partner):
@@ -86,6 +86,8 @@
     flux_ref,
     e1_ref,
     e2_ref,
+    warm_rows,
+    picked_ref,
     aloft_ref,
     warm_ids_ref,
     cool_ids_ref,
@@ -97,6 +99,7 @@
     flux_out,
     flux_in,
     ext,
+    sea_waves,
     waves,
     waves_out,
     waves_in,
@@ -128,7 +131,9 @@
     fourier_recv,
     quad_send,
     quad_recv,
-    pass_send,
+    beside_send,
+    across_send,
+    again_send,
     pass_recv,
 ):
     (grps, lats, lons, lat_count, levels, lon_local, block_air, m_local, degrees, olev, rows, cols) = sizes
@@ -141,9 +146,11 @@
     line = lat_count * BLK_PAD
     lon_per, lat_per = lons // grps, lats // grps
     flux_owner, yy = y // lon_per, lax.rem(y, lon_per)
-    sea_owner, tt = t // lat_per, lax.rem(t, lat_per)
+    sea_owner, tt = lax.rem(t, grps), t // grps
     core = lax.rem(g, 2)
-    sibling = {"grp": g + 1 - 2 * core}
+    beside = g + 1 - 2 * core
+    across = lax.rem(g + 2, grps)
+    beyond = across + 1 - 2 * core
     north, south = shifted(t, lats - 1, lats), shifted(t, 1, lats)
     west, east = shifted(y, lons - 1, lons), shifted(y, 1, lons)
     mid_rows, mid_cols = slice(8, 8 + rows), slice(LANES, LANES + cols)
@@ -160,7 +167,7 @@
         ({"lat": north, "lon": east}, first_rows, high_rows, low_cols),
         ({"lat": north, "lon": west}, first_rows, high_rows, high_cols),
     ]
-    pairs = lats // 2
+    turns = lats // grps
 
     fetches = [
         pltpu.make_async_copy(src, dst, local_sems.at[k])
@@ -180,8 +187,8 @@
 
     stage[...] = heat_ref[0].astype(bf16)
     expected = jnp.where(g == 0, jnp.where(sea_owner == 0, lats - 1, lats), 0)
-    keepers = [(g * lat_per + k, {"grp": jnp.int32(0), "lat": g * lat_per + k}) for k in range(lat_per)]
-    greet(
+    keepers = [(k * grps + g, {"grp": jnp.int32(0), "lat": k * grps + g}) for k in range(lat_per)]
+    awaited = greet(
         [{"grp": shifted(g, d, grps)} for d in range(1, grps)]
         + [{"lon": shifted(y, d, lons)} for d in range(1, lons)]
         + [{"lat": shifted(t, d, lats)} for d in range(1, lats)]
@@ -190,40 +197,22 @@
         expected,
     )
 
-    @pl.when(g == 0)
-    def _():
-        for d in range(1, lats):
-            remote(
-                stage,
-                sea_ref.at[y, tt],
-                sea1_send.at[d],
-                sea1_recv.at[tt],
-                {"grp": sea_owner, "lat": shifted(t, d, lats)},
-            ).start()
-
-    @pl.when((g == 0) & (sea_owner != 0))
-    def _():
-        remote(
-            stage, sea_ref.at[y, tt], sea1_send.at[0], sea1_recv.at[tt], {"grp": sea_owner}
-        ).start()
-
-    @pl.when((g == 0) & (sea_owner == 0))
-    def _():
-        sea_ref[y, tt] = stage[...]
-
-    def offset_of(rank):
-        half = jnp.where(rank % 2 == 1, (rank + 1) // 2, pairs - rank // 2)
-        return 2 * lax.rem(half, pairs) + core
-
-    def pack(rank):
-        other = shifted(t, offset_of(rank), lats)
+    def distance(rank):
+        half = jnp.where(rank % 2 == 1, (rank + 1) // 2, turns - rank // 2)
+        return grps * lax.rem(half, turns)
+
+    def source(rank, member):
+        return shifted(t, lats - distance(rank) - member, lats)
+
+    def pack(rank, carry):
+        other = shifted(t, distance(rank) + g, lats)
         start = other * n_local
         first = jnp.minimum(start // LANES, degrees // LANES - 2)
         offset = start - first * LANES
         lanes = pl.ds(pl.multiple_of(first * LANES, LANES), 2 * LANES)
         at = lax.broadcasted_iota(i32, (16, 2 * LANES), 1)
 
-        def some_rows(b, carry):
+        def some_rows(b, inner_carry):
             own = pl.ds(pl.multiple_of(b * 16, 16), 16)
             out = [jnp.zeros((16, LANES), f32) for _ in range(lat_count * n_local // LANES + 1)]
             for i in range(lat_count):
@@ -236,57 +225,85 @@
                     out[tile + 1] = out[tile + 1] + window[:, LANES:]
             for k in range(lat_count * n_local // LANES):
                 quad_out[rank, own, k * LANES : (k + 1) * LANES] = out[k].astype(bf16)
-            return carry
+            return inner_carry
 
         lax.fori_loop(0, m_local // 16, some_rows, 0)
-
-    def quad_copy(rank):
-        return remote(
-            quad_out.at[rank],
-            quad_in.at[t],
-            quad_send.at[rank],
-            quad_recv.at[t],
-            {"lat": shifted(t, offset_of(rank), lats)},
-        )
+        return carry
 
     own_copy = pltpu.make_async_copy(quad_out.at[0], quad_in.at[t], own_sem)
 
-    def pack_and_send(rank, carry):
-        pack(rank)
-
-        @pl.when((rank == 0) & (core == 0))
+    def send_packed(rank, carry):
+        @pl.when((rank == 0) & (g == 0))
         def _():
             own_copy.start()
 
-        @pl.when((rank != 0) | (core != 0))
+        @pl.when((rank != 0) | (g != 0))
         def _():
-            quad_copy(rank).start()
+            remote(
+                quad_out.at[rank],
+                quad_in.at[t],
+                quad_send.at[rank],
+                quad_recv.at[t],
+                {"lat": shifted(t, distance(rank) + g, lats)},
+            ).start()
 
         return carry
 
-    def source(rank):
-        return shifted(t, lats - offset_of(rank), lats)
-
     def pass_on(rank, carry):
-        @pl.when((rank == 0) & (core == 0))
+        s = source(rank, g)
+
+        @pl.when((rank == 0) & (g == 0))
         def _():
             own_copy.wait()
 
-        @pl.when((rank != 0) | (core != 0))
+        @pl.when((rank != 0) | (g != 0))
         def _():
-            landed(quad_in.at[source(rank)], quad_recv.at[source(rank)])
+            landed(quad_in.at[s], quad_recv.at[s])
 
         remote(
-            quad_in.at[source(rank)],
-            quad_in.at[source(rank)],
-            pass_send.at[rank],
-            pass_recv.at[source(rank)],
-            sibling,
+            quad_in.at[s], quad_in.at[s], beside_send.at[rank], pass_recv.at[s], {"grp": beside}
+        ).start()
+        remote(
+            quad_in.at[s], quad_in.at[s], across_send.at[rank], pass_recv.at[s], {"grp": across}
         ).start()
         return carry
 
+    def pass_again(rank, carry):
+        s = source(rank, across)
+        landed(quad_in.at[s], pass_recv.at[s])
+        remote(
+            quad_in.at[s], quad_in.at[s], again_send.at[rank], pass_recv.at[s], {"grp": beside}
+        ).start()
+        return carry
+
     fetches[3].wait()
-    lax.fori_loop(0, pairs, pack_and_send, 0)
+    lax.fori_loop(0, turns // 2, pack, 0)
+    pl.semaphore_wait(pltpu.get_barrier_semaphore(), awaited)
+
+    @pl.when(g == 0)
+    def _():
+        for d in range(1, lats):
+            remote(
+                stage,
+                sea_ref.at[y, tt],
+                sea1_send.at[d],
+                sea1_recv.at[tt],
+                {"grp": sea_owner, "lat": shifted(t, d, lats)},
+            ).start()
+
+    @pl.when((g == 0) & (sea_owner != 0))
+    def _():
+        remote(
+            stage, sea_ref.at[y, tt], sea1_send.at[0], sea1_recv.at[tt], {"grp": sea_owner}
+        ).start()
+
+    @pl.when((g == 0) & (sea_owner == 0))
+    def _():
+        sea_ref[y, tt] = stage[...]
+
+    lax.fori_loop(0, turns // 2, send_packed, 0)
+    lax.fori_loop(turns // 2, turns, pack, 0)
+    lax.fori_loop(turns // 2, turns, send_packed, 0)
 
     for fetch in fetches[:3]:
         fetch.wait()
@@ -338,19 +355,22 @@
             part, gathered.at[g], flux0_send, flux0_recv.at[g], {"grp": flux_owner}
         ).start()
 
-    for k in range(lat_per):
-        @pl.when((g != 0) | (lat_per * g + k != t))
+    for r in range(lat_per):
+        nearest = (t - g + lats) // grps
+        k = lax.rem(nearest + lats + ((r + 1) // 2 if r % 2 else -(r // 2)), lat_per)
+
+        @pl.when((g != 0) | (k * grps + g != t))
         def _():
             landed(sea_ref.at[y, k], sea1_recv.at[k])
 
-    for d in range(1, lons):
-        remote(
-            sea_ref.at[y],
-            sea_ref.at[y],
-            sea2_send.at[d],
-            sea2_recv.at[y],
-            {"lon": shifted(y, d, lons)},
-        ).start()
+        for d in range(1, lons):
+            remote(
+                sea_ref.at[y, k],
+                sea_ref.at[y, k],
+                sea2_send.at[d * lat_per + r],
+                sea2_recv.at[y * lat_per + k],
+                {"lon": shifted(y, d, lons)},
+            ).start()
 
     for level in range(olev):
         ext[level, mid_rows, mid_cols] = heat_ref[level]
@@ -407,30 +427,17 @@
 
     lax.fori_loop(lat_count // 2, lat_count, tables, 0)
 
-    for k in range(lon_per):
-        @pl.when(g * lon_per + k != y)
-        def _():
-            landed(flux_ref.at[t, k], flux1_recv.at[k])
-
-    for d in range(1, lats):
-        remote(
-            flux_ref.at[t],
-            flux_ref.at[t],
-            flux2_send.at[d],
-            flux2_recv.at[t],
-            {"lat": shifted(t, d, lats)},
-        ).start()
-
-    for d in range(1, lons):
-        other = shifted(y, d, lons)
-        landed(sea_ref.at[other], sea2_recv.at[other])
-
-    count_rows = lons * lat_per * rows
-    table = sea_ref[...].reshape(count_rows, cols).astype(f32)
-    table = jnp.concatenate(
-        [jnp.transpose(table[k : k + LANES]) for k in range(0, count_rows, LANES)], axis=1
-    ).astype(bf16)
     picks = 2 * blocks
+    fill = jnp.zeros((picks, 8 - block_air, LANES), f32)
+    fetches[5].wait()
+
+    def prepare(i, carry):
+        factor = warm_ref[pl.ds(i * picks, picks)].astype(f32)
+        factor = jnp.concatenate([factor, fill], axis=1).reshape(picks * 8, LANES)
+        warm_rows[i] = factor.astype(bf16)
+        return carry
+
+    lax.fori_loop(0, lat_count, prepare, 0)
     warm_ids_ref[...] = jnp.full_like(warm_ids_ref, -1)
     for i in range(lat_count):
         for k in range(warm_raw_ref.shape[1]):
@@ -440,21 +447,36 @@
     chosen = warm_ids_ref[...]
     column, row = chosen % lons, chosen // lons
     band = row // rows
-    spot = (column * lat_per + band % lat_per) * rows + row % rows
-    spot = jnp.where((band // lat_per == g) & (chosen >= 0), spot, -1)
-    fetches[5].wait()
-    table_row = lax.broadcasted_iota(i32, (count_rows, LANES), 0)
+    spot = (band // grps) * rows + row % rows
+    spot = jnp.where((band % grps == g) & (chosen >= 0), spot + column * LANES, -1)
+    spot = jnp.concatenate([spot[i : i + 1] for i in range(lat_count)], axis=1)
+    table_row = lax.broadcasted_iota(i32, (LANES, lat_count * LANES), 0)
+
+    lax.fori_loop(0, turns // 2, pass_on, 0)
+
+    def pick_chunk(r, carry):
+        other = lax.rem(y + lons + jnp.where(r % 2 == 1, (r + 1) // 2, -(r // 2)), lons)
+
+        @pl.when(other != y)
+        def _():
+            for k in range(lat_per):
+                landed(sea_ref.at[other, k], sea2_recv.at[other * lat_per + k])
+
+        chunk = jnp.transpose(sea_ref[other].reshape(LANES, cols).astype(f32)).astype(bf16)
+        one_hot = jnp.where(table_row == spot - other * LANES, 1.0, 0.0).astype(bf16)
+        found = jnp.dot(chunk, one_hot, preferred_element_type=f32)
+        picked_ref[...] = jnp.where(r == 0, found, picked_ref[...] + found)
+        return carry
+
+    picked_ref[...] = jnp.zeros_like(picked_ref)
+    lax.fori_loop(0, lons, pick_chunk, 0)
     pick_id = lax.broadcasted_iota(i32, (picks, 8, LANES), 0)
     pick_lane = lax.broadcasted_iota(i32, (picks, 8, LANES), 2)
     diagonal = pick_lane == (pick_id % 2) * BLK_PAD + pick_id // 2
-    fill = jnp.zeros((picks, 8 - block_air, LANES), f32)
     warm_sums = []
     for i in range(lat_count):
-        one_hot = jnp.where(table_row == spot[i : i + 1, :], 1.0, 0.0).astype(bf16)
-        picked = jnp.dot(table, one_hot, preferred_element_type=f32).astype(bf16)
-        factor = warm_ref[picks * i : picks * (i + 1)].astype(f32)
-        factor = jnp.concatenate([factor, fill], axis=1).reshape(picks * 8, LANES).astype(bf16)
-        product = jnp.dot(factor, picked, preferred_element_type=f32)
+        picked = picked_ref[:, i * LANES : (i + 1) * LANES].astype(bf16)
+        product = jnp.dot(warm_rows[i], picked, preferred_element_type=f32)
         product = product.reshape(picks, 8, LANES)
         total = jnp.sum(jnp.where(diagonal, product, 0.0), axis=0)
         warm_sums.append(total + pltpu.roll(total, BLK_PAD, 1))
@@ -471,39 +493,57 @@
             {"grp": shifted(g, d, grps)},
         ).start()
 
-    warmth_in[g] = warmth_out[...]
+    for k in range(lon_per):
+        @pl.when(g * lon_per + k != y)
+        def _():
+            landed(flux_ref.at[t, k], flux1_recv.at[k])
+
+    for d in range(1, lats):
+        remote(
+            flux_ref.at[t],
+            flux_ref.at[t],
+            flux2_send.at[d],
+            flux2_recv.at[t],
+            {"lat": shifted(t, d, lats)},
+        ).start()
+
+    def transform(field, count, out_ref):
+        lane = lax.broadcasted_iota(i32, field.shape, 1)
+        stacked = jnp.concatenate(
+            [jnp.where(lane // BLK_PAD == i, field, 0.0) for i in range(lat_count)], axis=0
+        ).astype(bf16)
+        real = jnp.dot(stacked, e1_ref[:, :wide], preferred_element_type=f32)
+        imag = jnp.dot(stacked, e1_ref[:, wide:], preferred_element_type=f32)
+        for i in range(lat_count):
+            slot_r = e2_ref[8 * i : 8 * i + 8, :wide]
+            slot_i = e2_ref[8 * i : 8 * i + 8, wide:]
+            for l in range(count):
+                at = (i * count + l) * 8
+                re, im = real[at : at + 8], imag[at : at + 8]
+                out_r = jnp.sum(re * slot_r - im * slot_i, axis=0, keepdims=True)
+                out_i = jnp.sum(re * slot_i + im * slot_r, axis=0, keepdims=True)
+                for c, out in enumerate((out_r, out_i)):
+                    row = (2 * l + c) * lat_count + i
+                    for k in range(lons):
+                        out_ref[k, row : row + 1, :] = out[:, k * LANES : (k + 1) * LANES]
+
+    transform(
+        jnp.concatenate(
+            [jnp.where(live, aloft_ref[8 * l : 8 * l + 8, :], 0.0) for l in range(levels)], axis=0
+        ),
+        levels,
+        waves,
+    )
+    lax.fori_loop(turns // 2, turns, pass_on, 0)
+    warmth = warmth_out[...]
     for d in range(1, grps):
         other = shifted(g, d, grps)
         landed(warmth_in.at[other], warmth_recv.at[other])
-    warmth = warmth_in[0]
-    for other in range(1, grps):
         warmth = warmth + warmth_in[other]
-    forced = jnp.concatenate(
-        [
-            jnp.where(live, aloft_ref[8 * l : 8 * l + 8, :] + sens_ref[l] * warmth, 0.0)
-            for l in range(levels)
-        ],
-        axis=0,
-    )
-    lane = lax.broadcasted_iota(i32, forced.shape, 1)
-    stacked = jnp.concatenate(
-        [jnp.where(lane // BLK_PAD == i, forced, 0.0) for i in range(lat_count)], axis=0
-    ).astype(bf16)
-    real = jnp.dot(stacked, e1_ref[:, :wide], preferred_element_type=f32)
-    imag = jnp.dot(stacked, e1_ref[:, wide:], preferred_element_type=f32)
-    for i in range(lat_count):
-        slot_r = e2_ref[8 * i : 8 * i + 8, :wide]
-        slot_i = e2_ref[8 * i : 8 * i + 8, wide:]
-        for l in range(levels):
-            at = (i * levels + l) * 8
-            re, im = real[at : at + 8], imag[at : at + 8]
-            out_r = jnp.sum(re * slot_r - im * slot_i, axis=0, keepdims=True)
-            out_i = jnp.sum(re * slot_i + im * slot_r, axis=0, keepdims=True)
-            for c, out in enumerate((out_r, out_i)):
-                row = (2 * l + c) * lat_count + i
-                for k in range(lons):
-                    waves[k, row : row + 1, :] = out[:, k * LANES : (k + 1) * LANES]
-
+    transform(jnp.where(live, warmth, 0.0), 1, sea_waves)
+    for l in range(levels):
+        at = slice(2 * l * lat_count, 2 * (l + 1) * lat_count)
+        waves[:, at, :] = waves[:, at, :] + sens_ref[l] * sea_waves[...]
     waves_out[...] = waves[...].astype(bf16)
     for d in range(1, lons):
         other = shifted(y, d, lons)
@@ -568,7 +608,7 @@
             flux_out, flux_in.at[g], fluxp_send, fluxp_recv.at[g], {"grp": jnp.int32(0)}
         ).start()
 
-    lax.fori_loop(0, pairs // 2, pass_on, 0)
+    lax.fori_loop(0, turns // 2, pass_again, 0)
 
     total = waves[y]
     for d in range(1, lons):
@@ -588,16 +628,12 @@
                 {"lat": shifted(t, offset, lats)},
             ).start()
 
-    def send_near(rank, carry):
-        send_fourier(offset_of(rank))
+    def send_some(rank, carry):
+        for member in range(grps):
+            send_fourier(distance(rank) + member)
         return carry
 
-    def send_far(rank, carry):
-        send_fourier(offset_of(rank) + 1 - 2 * core)
-        return carry
-
-    lax.fori_loop(0, pairs, send_near, 0)
-    lax.fori_loop(0, pairs, send_far, 0)
+    lax.fori_loop(0, turns, send_some, 0)
 
     @pl.when(g == 0)
     def _():
@@ -616,7 +652,7 @@
             partner,
         ).start()
 
-    lax.fori_loop(pairs // 2, pairs, pass_on, 0)
+    lax.fori_loop(turns // 2, turns, pass_again, 0)
 
     span = lat_count * n_local
     repeat_row = lax.broadcasted_iota(i32, (LANES, span), 0)
@@ -630,7 +666,7 @@
     part_lane = lax.broadcasted_iota(i32, (m_local, LANES), 1) // lat_count
     sums[...] = jnp.zeros_like(sums)
 
-    def add_source(s):
+    def coefficients(s):
         @pl.when(s != t)
         def _():
             landed(fourier.at[s], fourier_recv.at[s])
@@ -639,23 +675,24 @@
         own = jnp.concatenate(
             [jnp.where(part_lane == a, columns, 0.0) for a in range(parts)], axis=0
         ).astype(bf16)
-        coef = jnp.dot(own, repeat, preferred_element_type=f32)
-        quad = quad_in[s].astype(f32)
+        return jnp.dot(own, repeat, preferred_element_type=f32)
+
+    def add_two(first, second):
+        coefs = coefficients(first), coefficients(second)
+        quads = quad_in[first].astype(f32), quad_in[second].astype(f32)
         for a in range(parts):
             at = slice(a * m_local, (a + 1) * m_local)
-            sums[at, :] = sums[at, :] + coef[at] * quad
-
-    def add_direct(rank, carry):
-        add_source(source(rank))
+            sums[at, :] = sums[at, :] + coefs[0][at] * quads[0] + coefs[1][at] * quads[1]
+
+    def add_some(rank, carry):
+        add_two(source(rank, g), source(rank, across))
+        for member in (beside, beyond):
+            s = source(rank, member)
+            landed(quad_in.at[s], pass_recv.at[s])
+        add_two(source(rank, beside), source(rank, beyond))
         return carry
 
-    def add_passed(rank, carry):
-        s = shifted(source(rank), lats - 1 + 2 * core, lats)
-        landed(quad_in.at[s], pass_recv.at[s])
-        add_source(s)
-        return carry
-
-    lax.fori_loop(0, pairs, add_direct, 0)
+    lax.fori_loop(0, 3 * turns // 4, add_some, 0)
 
     for index, (partner, src_rows, dst_rows, dst_cols) in enumerate(halo):
         landed(ext.at[:, dst_rows, dst_cols], halo_recv.at[index])
@@ -675,7 +712,7 @@
             field = field + KAPPA * wet * total
         ocean_ref[level] = field[mid_rows, mid_cols]
 
-    lax.fori_loop(0, pairs, add_passed, 0)
+    lax.fori_loop(3 * turns // 4, turns, add_some, 0)
 
     folded = jnp.zeros((parts * m_local, LANES), f32)
     for i in range(lat_count):
@@ -721,7 +758,8 @@
         landed(flux_ref.at[t], flux2_send.at[d])
         landed(fourier.at[t], fourier_send.at[d])
     for d in range(1, lons):
-        landed(sea_ref.at[y], sea2_send.at[d])
+        for r in range(lat_per):
+            landed(sea_ref.at[y, 0], sea2_send.at[d * lat_per + r])
         landed(waves_out.at[0], waves_send.at[d])
     for d in range(1, grps):
         landed(warmth_out, warmth_send.at[d])
@@ -729,14 +767,15 @@
         landed(ext.at[:, src_rows, mid_cols], halo_send.at[index])
 
     def sent(rank, carry):
-        @pl.when((rank != 0) | (core != 0))
+        @pl.when((rank != 0) | (g != 0))
         def _():
             landed(quad_out.at[rank], quad_send.at[rank])
 
-        landed(quad_in.at[0], pass_send.at[rank])
+        for sem in (beside_send, across_send, again_send):
+            landed(quad_in.at[0], sem.at[rank])
         return carry
 
-    lax.fori_loop(0, pairs, sent, 0)
+    lax.fori_loop(0, turns, sent, 0)
 
 
 def per_device(
@@ -797,6 +836,8 @@
             pltpu.VMEM((lats, lon_per, line // 16, LANES), bf16),
             pltpu.VMEM((line, 2 * wide), bf16),
             pltpu.VMEM((lat_count * 8, 2 * wide), f32),
+            pltpu.VMEM((lat_count, blocks * warm_ways * 8, cols), bf16),
+            pltpu.VMEM((cols, lat_count * LANES), f32),
             pltpu.VMEM((levels * 8, line), f32),
             pltpu.VMEM((lat_count, warm_ways * BLK_PAD), jnp.int32),
             pltpu.VMEM((8, rows * cool_ways), jnp.int32),
@@ -808,11 +849,12 @@
             pltpu.VMEM((rows, cols), f32),
             pltpu.VMEM((grps, rows, cols), f32),
             pltpu.VMEM((olev + 1, rows + 16, cols + 2 * LANES), f32),
+            pltpu.VMEM((lons, 2 * lat_count, LANES), f32),
             pltpu.VMEM((lons, parts * lat_count, LANES), f32),
             pltpu.VMEM((lons, parts * lat_count, LANES), bf16),
             pltpu.VMEM((lons, parts * lat_count, LANES), bf16),
             pltpu.VMEM((lats, parts * lat_count, LANES), bf16),
-            pltpu.VMEM((lats // 2, m_local, lat_count * n_local), bf16),
+            pltpu.VMEM((lats // grps, m_local, lat_count * n_local), bf16),
             pltpu.VMEM((lats, m_local, lat_count * n_local), bf16),
             pltpu.VMEM((parts * m_local, lat_count * n_local), f32),
             dmas(6),
@@ -823,8 +865,8 @@
             dmas(grps),
             dmas(lons),
             dmas(lon_per),
-            dmas(lons),
-            dmas(lons),
+            dmas(lons * lat_per),
+            dmas(lons * lat_per),
             dmas(lats),
             dmas(lats),
             dmas(grps),
@@ -837,9 +879,11 @@
             dmas(lons),
             dmas(lats),
             dmas(lats),
-            dmas(lats // 2),
+            dmas(lats // grps),
             dmas(lats),
-            dmas(lats // 2),
+            dmas(lats // grps),
+            dmas(lats // grps),
+            dmas(lats // grps),
             dmas(lats),
         ],
         compiler_params=pltpu.CompilerParams(

time: 62 us -> 60.6 us (0.977)
  the two profiles are of different devices: /device:TPU:122 before, /device:TPU:6 now
where the time goes in v4:
time: 60.6 us; the launch traced here: 59.5 us
  Pallas kernels  55.4 us (91%)
  local copies, waits for them, and re-layouts  3.36 us (6%)
  between operations  0.77 us (1%)
    pallas_call x1, Pallas kernels, per_device(): pl.pallas_call(functools.partial(step_kernel, sizes), out_shape=(jax.Shap...  55.4 us
    unnamed x22, local copies, waits for them, and re-layouts  2.55 us

profile of v4, /device:TPU:6, one launch (start us, length us, event | category | flops | bytes accessed | tf_op | source)
XLA Modules:
  0.0 59.5 jit_solution(9221376949604806940)
XLA Ops:
  0.6 0.0 copy-start.5
  0.6 0.0 copy-start.1
  0.7 0.0 copy-start.6
  0.7 0.0 copy-start.3
  0.7 0.0 copy-start.2
  0.7 0.0 copy-start
  0.7 0.0 copy-start.9
  0.7 0.0 copy-start.8
  0.7 0.0 copy-start.7
  0.7 0.0 copy-start.4
  0.7 1.8 %copy.13 = bf16[8,54,2,6,128]{4,3,2,1,0:T(8,128)(2,1)S(1)} copy(bf16[8,54,2,6,128]{4,2,3,1,0:T(2,128)(2,1)} %param.21) | data formatting | bytes 2654208 | tf_op args[10]
  2.5 0.0 copy-done.5
  2.5 0.0 copy-done.1
  2.5 0.0 copy-done.6
  2.5 0.0 copy-done.3
  2.5 0.0 copy-done.2
  2.5 0.1 copy-done
  2.7 0.0 copy-done.9
  2.7 0.0 copy-done.8
  2.7 0.0 copy-done.7
  2.7 0.0 copy-done.4
  2.7 55.4 %shard_map.122 = (f32[80,384]{1,0:T(8,128)S(1)}, f32[4,32,128]{2,1,0:T(8,128)S(1)}) custom-call(s32[8]{0:T(128)S(1)} %copy-done.7, f32[2]{0:T(128)S(1)} %copy-done.8, f32[2]{0:T(128)S(1)} %copy-done.9, bf16[8,80,1280]{2,1,0:T(8,128)(2,1)S(1)} %copy-done, bf16[864,6,128]{2,1,0:T(8,128)(2,1)S(1)} %bitcast.9, bf16[192,4,128]{2,1,0:T(4,128)(2,1)S(1)} %bitcast.10, ...), custom_call_target="tpu_custom_call" | custom-call | tf_op jit(solution)/shard_map/pallas_call | solution.py:820
  58.1 0.8 %reshape.15 = f32[80,4,80]{2,1,0:T(4,128)} reshape(f32[80,320]{1,0:T(8,128)S(1)} %bitcast.11) | data formatting | bytes 204800 | tf_op jit(solution)/shard_map/reshape | solution.py:905
  58.9 0.6 %copy.15 = f32[4,32,128]{2,1,0:T(8,128)} copy(f32[4,32,128]{2,1,0:T(8,128)S(1)} %get-tuple-element.9) | data formatting | bytes 131072
Async XLA Ops:
  0.6 1.9 %copy-start.5 = (s32[8,54,2]{1,2,0:T(2,128)S(1)}, s32[8,54,2]{1,2,0:T(2,128)}, u32[]{:S(2)}) copy-start(s32[8,54,2]{1,2,0:T(2,128)} %param.20) | copy-start | bytes 10372
  0.6 1.9 %copy-start.1 = (bf16[32,1,4,6,128]{4,2,3,1,0:T(4,128)(2,1)S(1)}, bf16[32,1,4,6,128]{4,2,3,1,0:T(4,128)(2,1)}, u32[]{:S(2)}) copy-start(bf16[32,1,4,6,128]{4,2,3,1,0:T(4,128)(2,1)} %param.19) | copy-start | bytes 589828
  0.7 1.9 %copy-start.6 = (s32[32,1,4]{0,2,1:T(4,128)S(1)}, s32[32,1,4]{0,2,1:T(4,128)}, u32[]{:S(2)}) copy-start(s32[32,1,4]{0,2,1:T(4,128)} %param.18) | copy-start | bytes 1540
  0.7 1.9 %copy-start.3 = (s32[32,128]{1,0:T(8,128)S(1)}, s32[32,128]{1,0:T(8,128)}, u32[]{:S(2)}) copy-start(s32[32,128]{1,0:T(8,128)} %water_ref.1) | copy-start | bytes 49156
  0.7 1.9 %copy-start.2 = (f32[4,32,128]{2,1,0:T(8,128)S(1)}, f32[4,32,128]{2,1,0:T(8,128)}, u32[]{:S(2)}) copy-start(f32[4,32,128]{2,1,0:T(8,128)} %heat_ref.1) | copy-start | bytes 196612
  0.7 2.0 %copy-start = (bf16[8,80,1280]{2,1,0:T(8,128)(2,1)S(1)}, bf16[8,80,1280]{2,1,0:T(8,128)(2,1)}, u32[]{:S(2)}) copy-start(bf16[8,80,1280]{2,1,0:T(8,128)(2,1)} %quad_hbm.1) | copy-start | bytes 4915204
  0.7 2.0 %copy-start.9 = (f32[2]{0:T(128)S(1)}, f32[2]{0:T(128)}, u32[]{:S(2)}) copy-start(f32[2]{0:T(128)} %sens_hbm.1) | copy-start | bytes 28
  0.7 2.0 %copy-start.8 = (f32[2]{0:T(128)S(1)}, f32[2]{0:T(128)}, u32[]{:S(2)}) copy-start(f32[2]{0:T(128)} %share_hbm.1) | copy-start | bytes 28
  0.7 2.0 %copy-start.7 = (s32[8]{0:T(128)S(1)}, s32[8]{0:T(128)}, u32[]{:S(2)}) copy-start(s32[8]{0:T(128)} %nodes_hbm.1) | copy-start | bytes 100
  0.7 2.0 %copy-start.4 = (bf16[2,8,324]{2,1,0:T(8,128)(2,1)S(1)}, bf16[2,8,324]{2,1,0:T(8,128)(2,1)}, u32[]{:S(2)}) copy-start(bf16[2,8,324]{2,1,0:T(8,128)(2,1)} %aloft_raw_ref.1) | copy-start | bytes 31108

commit v5 on v4

--- a/solution.py
+++ b/solution.py
@@ -635,6 +635,8 @@
 
     lax.fori_loop(0, turns, send_some, 0)
 
+    lax.fori_loop(turns // 2, turns, pass_again, 0)
+
     @pl.when(g == 0)
     def _():
         total = flux_out[...]
@@ -652,7 +654,6 @@
             partner,
         ).start()
 
-    lax.fori_loop(turns // 2, turns, pass_again, 0)
 
     span = lat_count * n_local
     repeat_row = lax.broadcasted_iota(i32, (LANES, span), 0)

time: 60.6 us -> 60.6 us (level)
  no operation moved by 1% of the time
where the time goes in v5:
time: 60.6 us; the launch traced here: 59.5 us
  Pallas kernels  55.4 us (91%)
  local copies, waits for them, and re-layouts  3.36 us (6%)
  between operations  0.77 us (1%)
    pallas_call x1, Pallas kernels, per_device(): pl.pallas_call(functools.partial(step_kernel, sizes), out_shape=(jax.Shap...  55.4 us
    unnamed x22, local copies, waits for them, and re-layouts  2.55 us

profile of v5, /device:TPU:6, one launch (start us, length us, event | category | flops | bytes accessed | tf_op | source)
XLA Modules:
  0.0 59.5 jit_solution(5388566294086254521)
XLA Ops:
  0.6 0.0 copy-start.5
  0.6 0.0 copy-start.1
  0.7 0.0 copy-start.6
  0.7 0.0 copy-start.3
  0.7 0.0 copy-start.2
  0.7 0.0 copy-start
  0.7 0.0 copy-start.9
  0.7 0.0 copy-start.8
  0.7 0.0 copy-start.7
  0.7 0.0 copy-start.4
  0.7 1.8 %copy.13 = bf16[8,54,2,6,128]{4,3,2,1,0:T(8,128)(2,1)S(1)} copy(bf16[8,54,2,6,128]{4,2,3,1,0:T(2,128)(2,1)} %param.21) | data formatting | bytes 2654208 | tf_op args[10]
  2.5 0.0 copy-done.5
  2.5 0.0 copy-done.1
  2.5 0.0 copy-done.6
  2.5 0.0 copy-done.3
  2.5 0.0 copy-done.2
  2.5 0.1 copy-done
  2.7 0.0 copy-done.9
  2.7 0.0 copy-done.8
  2.7 0.0 copy-done.7
  2.7 0.0 copy-done.4
  2.7 55.4 %shard_map.122 = (f32[80,384]{1,0:T(8,128)S(1)}, f32[4,32,128]{2,1,0:T(8,128)S(1)}) custom-call(s32[8]{0:T(128)S(1)} %copy-done.7, f32[2]{0:T(128)S(1)} %copy-done.8, f32[2]{0:T(128)S(1)} %copy-done.9, bf16[8,80,1280]{2,1,0:T(8,128)(2,1)S(1)} %copy-done, bf16[864,6,128]{2,1,0:T(8,128)(2,1)S(1)} %bitcast.9, bf16[192,4,128]{2,1,0:T(4,128)(2,1)S(1)} %bitcast.10, ...), custom_call_target="tpu_custom_call" | custom-call | tf_op jit(solution)/shard_map/pallas_call | solution.py:821
  58.1 0.8 %reshape.15 = f32[80,4,80]{2,1,0:T(4,128)} reshape(f32[80,320]{1,0:T(8,128)S(1)} %bitcast.11) | data formatting | bytes 204800 | tf_op jit(solution)/shard_map/reshape | solution.py:906
  58.9 0.6 %copy.15 = f32[4,32,128]{2,1,0:T(8,128)} copy(f32[4,32,128]{2,1,0:T(8,128)S(1)} %get-tuple-element.9) | data formatting | bytes 131072
Async XLA Ops:
  0.6 1.9 %copy-start.5 = (s32[8,54,2]{1,2,0:T(2,128)S(1)}, s32[8,54,2]{1,2,0:T(2,128)}, u32[]{:S(2)}) copy-start(s32[8,54,2]{1,2,0:T(2,128)} %param.20) | copy-start | bytes 10372
  0.6 1.9 %copy-start.1 = (bf16[32,1,4,6,128]{4,2,3,1,0:T(4,128)(2,1)S(1)}, bf16[32,1,4,6,128]{4,2,3,1,0:T(4,128)(2,1)}, u32[]{:S(2)}) copy-start(bf16[32,1,4,6,128]{4,2,3,1,0:T(4,128)(2,1)} %param.19) | copy-start | bytes 589828
  0.7 1.9 %copy-start.6 = (s32[32,1,4]{0,2,1:T(4,128)S(1)}, s32[32,1,4]{0,2,1:T(4,128)}, u32[]{:S(2)}) copy-start(s32[32,1,4]{0,2,1:T(4,128)} %param.18) | copy-start | bytes 1540
  0.7 1.9 %copy-start.3 = (s32[32,128]{1,0:T(8,128)S(1)}, s32[32,128]{1,0:T(8,128)}, u32[]{:S(2)}) copy-start(s32[32,128]{1,0:T(8,128)} %water_ref.1) | copy-start | bytes 49156
  0.7 1.9 %copy-start.2 = (f32[4,32,128]{2,1,0:T(8,128)S(1)}, f32[4,32,128]{2,1,0:T(8,128)}, u32[]{:S(2)}) copy-start(f32[4,32,128]{2,1,0:T(8,128)} %heat_ref.1) | copy-start | bytes 196612
  0.7 2.0 %copy-start = (bf16[8,80,1280]{2,1,0:T(8,128)(2,1)S(1)}, bf16[8,80,1280]{2,1,0:T(8,128)(2,1)}, u32[]{:S(2)}) copy-start(bf16[8,80,1280]{2,1,0:T(8,128)(2,1)} %quad_hbm.1) | copy-start | bytes 4915204
  0.7 2.0 %copy-start.9 = (f32[2]{0:T(128)S(1)}, f32[2]{0:T(128)}, u32[]{:S(2)}) copy-start(f32[2]{0:T(128)} %sens_hbm.1) | copy-start | bytes 28
  0.7 2.0 %copy-start.8 = (f32[2]{0:T(128)S(1)}, f32[2]{0:T(128)}, u32[]{:S(2)}) copy-start(f32[2]{0:T(128)} %share_hbm.1) | copy-start | bytes 28
  0.7 2.0 %copy-start.7 = (s32[8]{0:T(128)S(1)}, s32[8]{0:T(128)}, u32[]{:S(2)}) copy-start(s32[8]{0:T(128)} %nodes_hbm.1) | copy-start | bytes 100
  0.7 2.0 %copy-start.4 = (bf16[2,8,324]{2,1,0:T(8,128)(2,1)S(1)}, bf16[2,8,324]{2,1,0:T(8,128)(2,1)}, u32[]{:S(2)}) copy-start(bf16[2,8,324]{2,1,0:T(8,128)(2,1)} %aloft_raw_ref.1) | copy-start | bytes 31108
